TPU v7x, 128 devices: a whole 4x4x4 slice. The times are simulated.
128 devices in a mesh: rows: 16 (over z_lo, y, core), cols: 8 (over z_hi, x).
Axes of the slice: x: 4, y: 4, z: 4 (z_hi: 2, z_lo: 2; z = z_hi * 2 + z_lo), core: 2. Of those that a mesh axis runs over, the one named last changes fastest.
Arguments:
- features: bfloat16 [256, 768, 512], P('rows', 'cols'), may hold values from -6 to 6
- conv_taps: float32 [9, 512], replicated, may hold values from -2 to 2
- block_gain: float32 [512], replicated, may hold values from 0.1 to 1.9
- block_qkv: bfloat16 [512, 1536], replicated, may hold values from -1.3258252 to 1.3258252
- block_out: bfloat16 [512, 512], replicated, may hold values from -0.25 to 0.25
- grid_gain: float32 [512], replicated, may hold values from 0.1 to 1.9
- grid_qkv: bfloat16 [512, 1536], replicated, may hold values from -1.3258252 to 1.3258252
- grid_out: bfloat16 [512, 512], replicated, may hold values from -0.25 to 0.25
Outputs:
- encoded: bfloat16 [256, 768, 512], P('rows', 'cols')
All inputs are finite; a program needn't handle non-finite values.
Results may differ from a plain program's by a relative error of at most 0.009.
Values may be sent and summed in bfloat16 or wider, within the bound.
A program may use at most 128 MiB of HBM per device.

v0:
```python
import jax
import jax.numpy as jnp
from jax import lax
from jax.sharding import PartitionSpec as P

HEADS = 16
BLOCK = 8
GRID = 8


def with_halo(cells, sides, width):
    for axis, dim in sides:
        count = lax.axis_size(axis)
        ends = count - 1
        head = lax.slice_in_dim(cells, 0, width, axis=dim)
        tail = lax.slice_in_dim(cells, cells.shape[dim] - width, cells.shape[dim], axis=dim)
        cells = jnp.concatenate(
            [
                lax.ppermute(tail, axis, [(i, (i + 1) % count) for i in range(ends)]),
                cells,
                lax.ppermute(head, axis, [((i + 1) % count, i) for i in range(ends)]),
            ],
            axis=dim,
        )
    return cells


def window_attention(windows, gain, w_qkv, w_out):
    count, length, channels = windows.shape
    head_dim = channels // HEADS
    wide = windows.astype(jnp.float32)
    average = jnp.mean(wide, axis=-1, keepdims=True)
    centred = wide - average
    spread = jnp.mean(centred * centred, axis=-1, keepdims=True)
    normed = (centred * lax.rsqrt(spread + 1e-05) * gain).astype(jnp.bfloat16)
    projected = jnp.dot(
        normed.reshape(count * length, channels), w_qkv, preferred_element_type=jnp.float32
    )
    projected = projected.astype(jnp.bfloat16).reshape(count, length, 3, HEADS, head_dim)
    queries = projected[:, :, 0]
    keys_all = projected[:, :, 1]
    values_all = projected[:, :, 2]
    scores = jnp.einsum(
        "nqhe,nkhe->nhqk", queries, keys_all, preferred_element_type=jnp.float32
    ) * head_dim ** (-0.5)
    weights_soft = jax.nn.softmax(scores, axis=-1).astype(jnp.bfloat16)
    attended = jnp.einsum(
        "nhqk,nkhe->nqhe", weights_soft, values_all, preferred_element_type=jnp.float32
    ).astype(jnp.bfloat16)
    output = jnp.dot(
        attended.reshape(count * length, channels), w_out, preferred_element_type=jnp.float32
    )
    return (output.reshape(count, length, channels) + wide).astype(jnp.bfloat16)


def body(features, conv_taps, block_gain, block_qkv, block_out, grid_gain, grid_qkv, grid_out):
    rows_n = lax.axis_size("rows")
    cols_n = lax.axis_size("cols")
    strip_rows, strip_cols, channels = features.shape
    padded = with_halo(features, (("rows", 0), ("cols", 1)), 1)
    wide = features.astype(jnp.float32)
    filtered = wide
    for tap_index in range(9):
        row_off = tap_index // 3
        col_off = tap_index % 3
        window_part = padded[row_off : row_off + strip_rows, col_off : col_off + strip_cols]
        filtered = filtered + conv_taps[tap_index] * window_part.astype(jnp.float32)
    convolved = filtered.astype(jnp.bfloat16)
    blocks = convolved.reshape(strip_rows // BLOCK, BLOCK, strip_cols // BLOCK, BLOCK, channels)
    blocks = blocks.transpose(0, 2, 1, 3, 4).reshape(-1, BLOCK * BLOCK, channels)
    blocked = window_attention(blocks, block_gain, block_qkv, block_out)
    blocked = blocked.reshape(strip_rows // BLOCK, strip_cols // BLOCK, BLOCK, BLOCK, channels)
    blocked = blocked.transpose(0, 2, 1, 3, 4).reshape(strip_rows, strip_cols, channels)
    row_piece = strip_rows // rows_n
    col_piece = strip_cols // GRID
    per_col = GRID // cols_n
    classes = rows_n // GRID
    sectioned = blocked.reshape(rows_n, row_piece, per_col, cols_n, col_piece, channels)
    arrived = lax.all_to_all(
        lax.all_to_all(sectioned, "rows", split_axis=0, concat_axis=0, tiled=True),
        "cols",
        split_axis=3,
        concat_axis=2,
        tiled=True,
    )
    grouped = arrived.reshape(rows_n, row_piece, GRID, col_piece, channels)
    spaced = grouped.reshape(GRID, classes, row_piece, GRID, col_piece, channels)
    windows = spaced.transpose(1, 2, 4, 0, 3, 5).reshape(-1, GRID * GRID, channels)
    gridded = window_attention(windows, grid_gain, grid_qkv, grid_out)
    gridded = gridded.reshape(classes, row_piece, col_piece, GRID, GRID, channels)
    gridded = gridded.transpose(3, 0, 1, 4, 2, 5).reshape(
        rows_n, row_piece, GRID, col_piece, channels
    )
    outgoing = gridded.reshape(rows_n, row_piece, GRID, 1, col_piece, channels)
    returned = lax.all_to_all(
        lax.all_to_all(outgoing, "rows", split_axis=0, concat_axis=0, tiled=True),
        "cols",
        split_axis=2,
        concat_axis=3,
        tiled=True,
    )
    encoded = returned.reshape(strip_rows, strip_cols, channels)
    return encoded


def solution(mesh):
    placed = (P("rows", "cols", None), P(), P(), P(), P(), P(), P(), P())
    return jax.shard_map(
        body, mesh=mesh, in_specs=placed, out_specs=P("rows", "cols", None), check_vma=False
    )
```

profile of v0, /device:TPU:1, one launch (start us, length us, event | category | flops | bytes accessed | tf_op | source)
XLA Modules:
  0.0 267.4 jit_solution(3987909983071924379)
XLA Ops:
  0.0 1.1 fusion.47
  1.1 4.6 %collective-permute-start = (bf16[1,96,512]{2,1,0:T(8,128)(2,1)S(1)}, bf16[1,96,512]{2,1,0:T(8,128)(2,1)S(1)}, u32[]{:S(2)}, u32[]{:S(2)}) collective-permute-start(bf16[1,96,512]{2,1,0:T(8,128)(2,1)S(1)} %get-tuple-element.14), channel_id=1, source_target_pairs={{0,8},{8,16},{16,24},{24,32},{32,40},{40,48},{48,56},{56,64},{64,7... | collective-permute-start | bytes 294920 | tf_op jit(solution)/shard_map/ppermute | solution.py:19
  5.7 1.9 collective-permute-start.1
  7.7 0.0 collective-permute-done
  7.7 1.5 constant_dynamic-update-slice_fusion.1
  9.2 2.4 collective-permute-done.1
  11.7 0.1 fusion.46
  11.7 3.1 %collective-permute-start.2 = (bf16[18,1,512]{2,1,0:T(2,128)(2,1)S(1)}, bf16[18,1,512]{2,1,0:T(2,128)(2,1)S(1)}, u32[]{:S(2)}, u32[]{:S(2)}) collective-permute-start(bf16[18,1,512]{2,1,0:T(2,128)(2,1)S(1)} %get-tuple-element.11), channel_id=1, source_target_pairs={{0,1},{1,2},{2,3},{3,4},{4,5},{5,6},{6,7},{8,9},{9,10},{10,11},{11... | collective-permute-start | bytes 55304 | tf_op jit(solution)/shard_map/ppermute | solution.py:19
  14.9 1.3 collective-permute-start.3
  16.2 0.0 collective-permute-done.2
  16.2 3.4 %collective-permute-done.3 = bf16[18,1,512]{2,1,0:T(2,128)(2,1)S(1)} collective-permute-done((bf16[18,1,512]{2,1,0:T(2,128)(2,1)S(1)}, bf16[18,1,512]{2,1,0:T(2,128)(2,1)S(1)}, u32[]{:S(2)}, u32[]{:S(2)}) %collective-permute-start.3) | collective-permute-done | bytes 18464 | tf_op jit(solution)/shard_map/ppermute | solution.py:21
  19.6 6.3 %fusion.20 = bf16[16,96,512]{2,1,0:T(8,128)(2,1)S(1)} fusion(bf16[16,96,512]{2,1,0:T(8,128)(2,1)S(1)} %copy-done.5, bf16[18,96,512]{2,1,0:T(8,128)(2,1)S(1)} %constant_dynamic-update-slice_fusion, bf16[18,1,512]{2,1,0:T(2,128)(2,1)S(1)} %collective-permute-done.3, bf16[18,1,512]{2,1,0:T(2,128)(2,1)S(1)} %collective-permute-done.2, ...), kind=kLoop, calls=%fused_computation.26 | loop fusion | flops 40894464 | bytes 5167104 | tf_op jit(solution)/shard_map/convert_element_type | solution.py:68
  25.9 0.3 bitcast_reduce_fusion
  26.2 0.1 div.33
  26.3 0.0 copy-start.9
  26.3 0.7 fusion.30
  27.0 2.2 copy.89
  29.2 0.1 rsqrt.23
  29.3 0.0 copy-done.9
  29.3 2.4 fusion.25
  31.7 4.3 %convolution_convert_fusion.1 = bf16[1536,1536]{1,0:T(8,128)(2,1)} fusion(bf16[1536,512]{1,0:T(8,128)(2,1)S(1)} %fusion.25, bf16[512,1536]{1,0:T(8,128)(2,1)S(1)} %copy-done), kind=kOutput, calls=%fused_computation.11 | convolution fusion | flops 2418278400 | bytes 7864320 | tf_op jit(solution)/shard_map/dot_general | solution.py:36
  36.0 6.6 %copy.90 = bf16[1536,1536]{0,1:T(8,128)(2,1)} copy(bf16[1536,1536]{1,0:T(8,128)(2,1)} %convolution_convert_fusion.1) | data formatting | bytes 9437184 | tf_op jit(solution)/shard_map/convert_element_type | solution.py:39
  42.7 12.6 %reshape.145 = bf16[24,64,3,16,32]{1,0,4,3,2:T(8,128)(2,1)} reshape(bf16[1536,1536]{0,1:T(8,128)(2,1)} %copy.90) | data formatting | bytes 9437184 | tf_op jit(solution)/shard_map/reshape | solution.py:39
  55.3 4.6 %fusion.45 = (bf16[24,64,1,16,32]{1,0,4,3,2:T(8,128)(2,1)S(1)}, bf16[24,64,1,16,32]{1,0,4,3,2:T(8,128)(2,1)S(1)}, bf16[24,64,1,16,32]{1,0,4,3,2:T(8,128)(2,1)S(1)}) fusion(bf16[24,64,3,16,32]{1,0,4,3,2:T(8,128)(2,1)} %reshape.145), kind=kLoop, calls=%fused_computation.84 | loop fusion | bytes 9437184 | tf_op jit(solution)/shard_map/slice | solution.py:42
  59.9 5.6 %fusion.22 = f32[24,16,64,64]{2,3,1,0:T(8,128)} fusion(bf16[24,64,1,16,32]{1,0,4,3,2:T(8,128)(2,1)S(1)} %get-tuple-element.10, bf16[24,64,1,16,32]{1,0,4,3,2:T(8,128)(2,1)S(1)} %get-tuple-element.9), kind=kOutput, calls=%fused_computation.32 | convolution fusion | flops 100663296 | bytes 9437184 | tf_op jit(solution)/shard_map/nqhe,nkhe->nhqk/dot_general | solution.py:43
  65.5 16.3 %fusion.49 = (f32[24,16,64]{2,1,0:T(8,128)S(1)}, f32[24,16,64,64]{2,3,1,0:T(8,128)}) fusion(f32[24,16,64,64]{2,3,1,0:T(8,128)} %fusion.22), kind=kOutput, calls=%fused_computation.88 | output fusion | flops 6291519 | bytes 12681216 | tf_op jit(solution)/shard_map/sub | solution.py:46
  81.8 6.5 %fusion.32 = bf16[24,16,32,64]{3,2,1,0:T(8,128)(2,1)S(1)} fusion(f32[24,16,64,64]{2,3,1,0:T(8,128)} %get-tuple-element.25, f32[24,16,64]{2,1,0:T(8,128)S(1)} %get-tuple-element.24, bf16[24,64,1,16,32]{1,0,4,3,2:T(8,128)(2,1)S(1)} %get-tuple-element.8), kind=kOutput, calls=%fused_computation.56 | convolution fusion | flops 104595456 | bytes 9535488 | tf_op jit(solution)/shard_map/nhqk,nkhe->nqhe/dot_general | solution.py:47
  88.3 0.0 copy-done.2
  88.3 0.0 copy-done.6
  88.3 1.0 add_convert_fusion.1
  89.3 0.6 copy.96
  89.9 0.9 copy.97
  90.8 27.4 %all_to_all.28 = bf16[16,1,1,8,12,512]{5,3,4,2,1,0:T(8,128)(2,1)S(1)} all-to-all(bf16[16,1,1,8,12,512]{5,3,4,2,1,0:T(8,128)(2,1)S(1)} %copy.97), channel_id=1, replica_groups=mesh['rows'=16,'cols'=8] {'rows'}, dimensions={0} | all-to-all | bytes 3145728 | tf_op jit(solution)/shard_map/all_to_all | solution.py:80
  118.2 0.9 copy.98
  119.1 30.6 %all_to_all.29 = bf16[16,1,1,8,12,512]{5,0,4,2,1,3:T(8,128)(2,1)S(1)} all-to-all(bf16[16,1,1,8,12,512]{5,0,4,2,1,3:T(8,128)(2,1)S(1)} %copy.98), channel_id=1, replica_groups=mesh['rows'=16,'cols'=8] {'cols'}, dimensions={3} | all-to-all | bytes 3145728 | tf_op jit(solution)/shard_map/all_to_all | solution.py:79
  149.7 0.9 copy.99
  150.6 0.3 fusion.37
  150.9 0.1 copy_multiply_fusion.1
  151.0 0.1 div.38
  151.1 0.7 multiply_reduce_fusion.2
  151.8 0.1 fusion.41
  151.9 0.1 rsqrt.25
  152.0 0.4 convert_bitcast_fusion
  152.4 0.0 copy-start.10
  152.5 0.4 copy.100
  152.9 0.0 copy-start.3
  152.9 1.7 copy-done.3
  154.7 0.5 fusion.28
  155.2 0.9 copy-done.11
  156.1 4.3 %convolution_convert_fusion = bf16[1536,1536]{1,0:T(8,128)(2,1)} fusion(bf16[1536,512]{1,0:T(8,128)(2,1)S(1)} %fusion.28, bf16[512,1536]{1,0:T(8,128)(2,1)S(1)} %copy-done.11), kind=kOutput, calls=%fused_computation.10 | convolution fusion | flops 2418278400 | bytes 7864320 | tf_op jit(solution)/shard_map/dot_general | solution.py:36
  160.4 6.6 %copy.104 = bf16[1536,1536]{0,1:T(8,128)(2,1)} copy(bf16[1536,1536]{1,0:T(8,128)(2,1)} %convolution_convert_fusion) | data formatting | bytes 9437184 | tf_op jit(solution)/shard_map/convert_element_type | solution.py:39
  167.0 12.6 %reshape.147 = bf16[24,64,3,16,32]{1,0,4,3,2:T(8,128)(2,1)} reshape(bf16[1536,1536]{0,1:T(8,128)(2,1)} %copy.104) | data formatting | bytes 9437184 | tf_op jit(solution)/shard_map/reshape | solution.py:39
  179.6 4.6 %fusion.44 = (bf16[24,64,1,16,32]{1,0,4,3,2:T(8,128)(2,1)S(1)}, bf16[24,64,1,16,32]{1,0,4,3,2:T(8,128)(2,1)S(1)}, bf16[24,64,1,16,32]{1,0,4,3,2:T(8,128)(2,1)S(1)}) fusion(bf16[24,64,3,16,32]{1,0,4,3,2:T(8,128)(2,1)} %reshape.147), kind=kLoop, calls=%fused_computation.83 | loop fusion | bytes 9437184 | tf_op jit(solution)/shard_map/slice | solution.py:42
  184.2 5.6 %fusion.21 = f32[24,16,64,64]{2,3,1,0:T(8,128)} fusion(bf16[24,64,1,16,32]{1,0,4,3,2:T(8,128)(2,1)S(1)} %get-tuple-element.7, bf16[24,64,1,16,32]{1,0,4,3,2:T(8,128)(2,1)S(1)} %get-tuple-element.6), kind=kOutput, calls=%fused_computation.28 | convolution fusion | flops 100663296 | bytes 9437184 | tf_op jit(solution)/shard_map/nqhe,nkhe->nhqk/dot_general | solution.py:43
  189.8 16.3 %fusion.50 = (f32[24,16,64]{2,1,0:T(8,128)S(1)}, f32[24,16,64,64]{2,3,1,0:T(8,128)}) fusion(f32[24,16,64,64]{2,3,1,0:T(8,128)} %fusion.21), kind=kOutput, calls=%fused_computation.89 | output fusion | flops 6291519 | bytes 12681216 | tf_op jit(solution)/shard_map/sub | solution.py:46
  206.1 6.5 %fusion.31 = bf16[24,16,32,64]{3,2,1,0:T(8,128)(2,1)S(1)} fusion(f32[24,16,64,64]{2,3,1,0:T(8,128)} %get-tuple-element.27, f32[24,16,64]{2,1,0:T(8,128)S(1)} %get-tuple-element.26, bf16[24,64,1,16,32]{1,0,4,3,2:T(8,128)(2,1)S(1)} %get-tuple-element.5), kind=kOutput, calls=%fused_computation.55 | convolution fusion | flops 104595456 | bytes 9535488 | tf_op jit(solution)/shard_map/nhqk,nkhe->nqhe/dot_general | solution.py:47
  212.6 0.0 copy-done.4
  212.6 0.0 copy-done.7
  212.6 1.0 add_convert_fusion
  213.7 0.1 copy.111
  213.8 26.4 %all_to_all.30 = bf16[16,1,8,1,12,512]{5,2,4,3,1,0:T(8,128)(2,1)S(1)} all-to-all(bf16[16,1,8,1,12,512]{5,2,4,3,1,0:T(8,128)(2,1)S(1)} %bitcast.124), channel_id=1, replica_groups=mesh['rows'=16,'cols'=8] {'rows'}, dimensions={0} | all-to-all | bytes 3145728 | tf_op jit(solution)/shard_map/all_to_all | solution.py:96
  240.2 0.9 copy.112
  241.1 24.3 %all_to_all.31 = bf16[16,1,8,1,12,512]{5,0,4,3,1,2:T(8,128)(2,1)S(1)} all-to-all(bf16[16,1,8,1,12,512]{5,0,4,3,1,2:T(8,128)(2,1)S(1)} %copy.112), channel_id=1, replica_groups=mesh['rows'=16,'cols'=8] {'cols'}, dimensions={2} | all-to-all | bytes 3145728 | tf_op jit(solution)/shard_map/all_to_all | solution.py:95
  265.4 2.0 copy.113
  (20 shorter events, 0.1 us)
Async XLA Ops:
  0.0 31.7 %copy-start = (bf16[512,1536]{1,0:T(8,128)(2,1)S(1)}, bf16[512,1536]{1,0:T(8,128)(2,1)}, u32[]{:S(2)}) copy-start(bf16[512,1536]{1,0:T(8,128)(2,1)} %param.11) | copy-start | bytes 4718596
  0.0 19.6 %copy-start.5 = (bf16[16,96,512]{2,1,0:T(8,128)(2,1)S(1)}, bf16[16,96,512]{2,1,0:T(8,128)(2,1)}, u32[]{:S(2)}) copy-start(bf16[16,96,512]{2,1,0:T(8,128)(2,1)} %param.8) | copy-start | bytes 4718596
  0.0 16.2 %copy-start.8 = (f32[9,512]{1,0:T(8,128)S(1)}, f32[9,512]{1,0:T(8,128)}, u32[]{:S(2)}) copy-start(f32[9,512]{1,0:T(8,128)} %param.9) | copy-start | bytes 55300
  1.1 6.5 %collective-permute-start = (bf16[1,96,512]{2,1,0:T(8,128)(2,1)S(1)}, bf16[1,96,512]{2,1,0:T(8,128)(2,1)S(1)}, u32[]{:S(2)}, u32[]{:S(2)}) collective-permute-start(bf16[1,96,512]{2,1,0:T(8,128)(2,1)S(1)} %get-tuple-element.14), channel_id=1, source_target_pairs={{0,8},{8,16},{16,24},{24,32},{32,40},{40,48},{48,56},{56,64},{64,7... | collective-permute-start | bytes 294920 | tf_op jit(solution)/shard_map/ppermute | solution.py:19
  5.7 5.9 %collective-permute-start.1 = (bf16[1,96,512]{2,1,0:T(8,128)(2,1)S(1)}, bf16[1,96,512]{2,1,0:T(8,128)(2,1)S(1)}, u32[]{:S(2)}, u32[]{:S(2)}) collective-permute-start(bf16[1,96,512]{2,1,0:T(8,128)(2,1)S(1)} %get-tuple-element.13), channel_id=1, source_target_pairs={{8,0},{16,8},{24,16},{32,24},{40,32},{48,40},{56,48},{64,56},{72,6... | collective-permute-start | bytes 294920 | tf_op jit(solution)/shard_map/ppermute | solution.py:21
  11.7 4.5 %collective-permute-start.2 = (bf16[18,1,512]{2,1,0:T(2,128)(2,1)S(1)}, bf16[18,1,512]{2,1,0:T(2,128)(2,1)S(1)}, u32[]{:S(2)}, u32[]{:S(2)}) collective-permute-start(bf16[18,1,512]{2,1,0:T(2,128)(2,1)S(1)} %get-tuple-element.11), channel_id=1, source_target_pairs={{0,1},{1,2},{2,3},{3,4},{4,5},{5,6},{6,7},{8,9},{9,10},{10,11},{11... | collective-permute-start | bytes 55304 | tf_op jit(solution)/shard_map/ppermute | solution.py:19
  14.9 4.7 %collective-permute-start.3 = (bf16[18,1,512]{2,1,0:T(2,128)(2,1)S(1)}, bf16[18,1,512]{2,1,0:T(2,128)(2,1)S(1)}, u32[]{:S(2)}, u32[]{:S(2)}) collective-permute-start(bf16[18,1,512]{2,1,0:T(2,128)(2,1)S(1)} %get-tuple-element.12), channel_id=1, source_target_pairs={{1,0},{2,1},{3,2},{4,3},{5,4},{6,5},{7,6},{9,8},{10,9},{11,10},{12... | collective-permute-start | bytes 55304 | tf_op jit(solution)/shard_map/ppermute | solution.py:21
  26.3 3.0 %copy-start.9 = (f32[512]{0:T(512)S(1)}, f32[512]{0:T(512)}, u32[]{:S(2)}) copy-start(f32[512]{0:T(512)} %param.10) | copy-start | bytes 6148
  81.8 6.5 %copy-start.2 = (f32[2,8,12,8,512]{4,3,1,2,0:T(8,128)S(1)}, f32[2,8,12,8,512]{4,3,1,2,0:T(8,128)}, u32[]{:S(2)}) copy-start(f32[2,8,12,8,512]{4,3,1,2,0:T(8,128)} %copy.89) | copy-start | bytes 9437188
  81.8 6.5 %copy-start.6 = (bf16[512,512]{1,0:T(8,128)(2,1)S(1)}, bf16[512,512]{1,0:T(8,128)(2,1)}, u32[]{:S(2)}) copy-start(bf16[512,512]{1,0:T(8,128)(2,1)} %param.12) | copy-start | bytes 1572868
  152.4 2.2 copy-start.10
  152.9 1.8 copy-start.3
  154.7 1.4 copy-start.11
  206.1 6.5 %copy-start.4 = (f32[2,1,12,8,8,512]{5,4,3,2,0,1:T(8,128)S(1)}, f32[2,1,12,8,8,512]{5,4,3,2,0,1:T(8,128)}, u32[]{:S(2)}) copy-start(f32[2,1,12,8,8,512]{5,4,3,2,0,1:T(8,128)} %copy-done.3) | copy-start | bytes 9437188
  206.1 6.5 %copy-start.7 = (bf16[512,512]{1,0:T(8,128)(2,1)S(1)}, bf16[512,512]{1,0:T(8,128)(2,1)}, u32[]{:S(2)}) copy-start(bf16[512,512]{1,0:T(8,128)(2,1)} %param.15) | copy-start | bytes 1572868
  240.2 27.2 %copy-start.1 = (bf16[512,1536]{1,0:T(8,128)(2,1)S(1)}, bf16[512,1536]{1,0:T(8,128)(2,1)}, u32[]{:S(2)}) copy-start(bf16[512,1536]{1,0:T(8,128)(2,1)} %param.11) | copy-start | bytes 4718596
where the time goes:
time: 270 us; the launch traced here: 267 us
  blocking collectives  109 us (40%)
  local copies, waits for them, and re-layouts  62.3 us (23%)
  other arithmetic  44.3 us (16%)
  matrix products  34.9 us (13%)
  starting transfers between devices  10.9 us (4%)
  waiting for transfers between devices  5.79 us (2%)
    sub x2, other arithmetic, window_attention(): weights_soft = jax.nn.softmax(scores, axis=-1).astype(jnp.bfloat16)  32.6 us
    all_to_all x1, blocking collectives, body(): lax.all_to_all(lax.all_to_all(sectioned, 'rows', split_axis=0, concat_axi...  30.6 us
    all_to_all x1, blocking collectives, body(): lax.all_to_all(sectioned, 'rows', split_axis=0, concat_axis=0, tiled=True)  27.4 us
    all_to_all x1, blocking collectives, body(): lax.all_to_all(outgoing, 'rows', split_axis=0, concat_axis=0, tiled=True)  26.4 us
    reshape x2, local copies, waits for them, and re-layouts, window_attention(): projected.astype(jnp.bfloat16).reshape(count, length, 3, HEADS, head_dim)  25.2 us
    all_to_all x1, blocking collectives, body(): lax.all_to_all(lax.all_to_all(outgoing, 'rows', split_axis=0, concat_axis...  24.3 us
    convert_element_type x2, local copies, waits for them, and re-layouts, window_attention(): projected.astype(jnp.bfloat16).reshape(count, length, 3, HEADS, head_dim)  13.3 us
    dot_general x2, matrix products, window_attention(): jnp.einsum('nhqk,nkhe->nqhe', weights_soft, values_all, preferred_element...  13 us
  transfers between devices with their start and end apart: 4, of which 2 were waited for; matrix products, arithmetic and copies ran while one was open for 1% of the time, Pallas kernels for 0%

commit v1 on v0

v1 whole, which is shorter than its diff:
```python
import jax
import jax.numpy as jnp
from jax import lax
from jax.experimental import pallas as pl
from jax.experimental.pallas import tpu as pltpu
from jax.sharding import PartitionSpec as P

MESH = pl.DeviceIdType.MESH
BF = jnp.bfloat16
F32 = jnp.float32
HEAD_DIM = 32
SCALE = HEAD_DIM ** -0.5
CHUNKS = 3
PEERS = 64
TOK = 512


def mm(a, b, dims=((1,), (0,))):
    return lax.dot_general(a, b, (dims, ((), ())), preferred_element_type=F32)


def norm_rows(x, gain):
    mean = jnp.mean(x, axis=-1, keepdims=True)
    cen = x - mean
    var = jnp.mean(cen * cen, axis=-1, keepdims=True)
    return (cen * lax.rsqrt(var + 1e-5) * gain).astype(BF)


def spread_heads(q):
    cols = []
    for h in range(4):
        parts = []
        if h > 0:
            parts.append(jnp.zeros((32 * h, 128), BF))
        parts.append(q[32 * h : 32 * (h + 1)])
        if h < 3:
            parts.append(jnp.zeros((32 * (3 - h), 128), BF))
        cols.append(jnp.concatenate(parts, axis=0))
    return jnp.concatenate(cols, axis=1)


def scores(unit, k_scr, qvt_scr):
    p, g = unit
    keys = k_scr[p * 128 : (p + 1) * 128, g * 128 : (g + 1) * 128]
    q = qvt_scr[g * 128 : (g + 1) * 128, p * 128 : (p + 1) * 128]
    s4 = mm(keys, spread_heads(q))
    first = lax.broadcasted_iota(jnp.int32, (64, 128), 1) < 64
    return [
        jnp.where(first, s4[:64, h * 128 : (h + 1) * 128], s4[64:, h * 128 : (h + 1) * 128])
        for h in range(4)
    ]


def soft(heads):
    lane = lax.broadcasted_iota(jnp.int32, (64, 128), 1)
    low = jnp.where(lane < 64, 1.0, 0.0).astype(BF)
    high = jnp.where(lane < 64, 0.0, 1.0).astype(BF)
    probs, inverse = [], []
    for s in heads:
        m = jnp.max(s, axis=0, keepdims=True)
        e = jnp.exp((s - m) * SCALE)
        inverse.append(1.0 / jnp.sum(e, axis=0, keepdims=True))
        pb = e.astype(BF)
        probs.append(jnp.concatenate([pb * low, pb * high], axis=0))
    return probs, inverse


def weigh(unit, softened, qvt_scr, ot_scr):
    p, g = unit
    probs, inverse = softened
    for h in range(0, 4, 2):
        r = g * 128 + h * 32
        v2 = qvt_scr[512 + r : 512 + r + 64, p * 128 : (p + 1) * 128]
        o2 = mm(v2, jnp.concatenate([probs[h], probs[h + 1]], axis=1))
        o = jnp.concatenate([o2[:32, :128] * inverse[h], o2[32:, 128:] * inverse[h + 1]], axis=0)
        ot_scr[r : r + 64, p * 128 : (p + 1) * 128] = o.astype(BF)


def attend(k_scr, qvt_scr, ot_scr):
    units = [(p, g) for p in range(4) for g in range(4)]
    n, b = len(units), 2
    ready = [scores(u, k_scr, qvt_scr) for u in units[:b]]
    last = None
    for i in range(0, n, b):
        now = ready
        if i + b < n:
            ready = [scores(u, k_scr, qvt_scr) for u in units[i + b : i + 2 * b]]
        done = [soft(s) for s in now]
        if last is not None:
            for u, x in zip(units[i - b : i], last):
                weigh(u, x, qvt_scr, ot_scr)
        last = done
    for u, x in zip(units[n - b :], last):
        weigh(u, x, qvt_scr, ot_scr)


def sublayer(n_scr, wk_scr, wqvt_scr, wo_scr, k_scr, qvt_scr, ot_scr):
    normed = n_scr[...]
    k_scr[...] = mm(normed, wk_scr[...]).astype(BF)
    qvt_scr[...] = mm(wqvt_scr[...], normed, ((1,), (1,))).astype(BF)
    attend(k_scr, qvt_scr, ot_scr)
    return mm(ot_scr[...], wo_scr[...], ((0,), (0,)))


def to_planes(x):
    y = x.reshape(PEERS, 8, 512)
    return jnp.concatenate([y[:, :, :256], y[:, :, 256:]], axis=1).astype(BF)


def from_planes(planes):
    y = planes.astype(F32)
    return jnp.concatenate([y[:, :8], y[:, 8:]], axis=2)


def main_kernel(
    feat_ref, taps_ref, bgain_ref, ggain_ref, bqkv_ref, bout_ref, gqkv_ref, gout_ref,
    ret_ref,
    fpad, coll, colr, lcol, rcol, x_scr, g_scr,
    bqkv, gqkv, bwo, gwo, wk_scr, wqvt_scr, n_scr, k_scr, qvt_scr, ot_scr,
    snd, rcv, snd2,
    local_sem, halo_send, halo_recv, ssem, rsem, ssem2, rsem2, own_sem,
):
    ri, ci = lax.axis_index("rows"), lax.axis_index("cols")
    core = lax.rem(ri, 2)
    me = (ri // 2) * 8 + ci
    up, down = lax.rem(ri + 15, 16), lax.rem(ri + 1, 16)
    left, right = lax.rem(ci + 7, 8), lax.rem(ci + 1, 8)

    load_feat = pltpu.make_async_copy(feat_ref, fpad.at[pl.ds(1, 16)], local_sem.at[0])
    load_feat.start()
    loads = [
        pltpu.make_async_copy(src, dst, local_sem.at[i + 1])
        for i, (src, dst) in enumerate(((bqkv_ref, bqkv), (bout_ref, bwo), (gqkv_ref, gqkv), (gout_ref, gwo)))
    ]
    for load in loads:
        load.start()

    def peer(d):
        t = lax.rem(me + d, PEERS)
        return t, (2 * (t // 8) + core, lax.rem(t, 8))

    barrier = pltpu.get_barrier_semaphore()

    def greet(d, carry):
        pl.semaphore_signal(barrier, inc=1, device_id=peer(d)[1], device_id_type=MESH)
        return carry

    around = [(r, c) for r in (up, down) for c in (left, ci, right)]
    for r, c in around:
        pl.semaphore_signal(barrier, inc=1, device_id=(r, c), device_id_type=MESH)
    lax.fori_loop(1, PEERS, greet, 0)

    load_feat.wait()
    for r in range(16):
        coll[r : r + 1, :] = fpad[r + 1, 0:1, :]
        colr[r : r + 1, :] = fpad[r + 1, 95:96, :]
    pl.semaphore_wait(barrier, PEERS - 1 + len(around))

    halo = [
        (fpad.at[1], fpad.at[17], (up, ci)),
        (fpad.at[16], fpad.at[0], (down, ci)),
        (coll, rcol.at[1], (ri, left)),
        (colr, lcol.at[1], (ri, right)),
        (coll, rcol.at[2], (up, left)),
        (coll, rcol.at[0], (down, left)),
        (colr, lcol.at[2], (up, right)),
        (colr, lcol.at[0], (down, right)),
    ]
    halo = [
        pltpu.make_async_remote_copy(
            src, dst, halo_send.at[i], halo_recv.at[i], device_id=to, device_id_type=MESH
        )
        for i, (src, dst, to) in enumerate(halo)
    ]
    for copy in halo:
        copy.start()

    def conv_row(r, above, below):
        half, rr = r // 8, lax.rem(r, 8)
        first = lax.broadcasted_iota(jnp.int32, (96, 128), 0) == 0
        last = lax.broadcasted_iota(jnp.int32, (96, 128), 0) == 95
        for lt in range(4):
            lanes = slice(lt * 128, (lt + 1) * 128)
            xm = fpad[r, :, lanes].astype(F32)
            x0 = fpad[r + 1, :, lanes].astype(F32)
            xp = fpad[r + 2, :, lanes].astype(F32)
            if above is not None:
                xm = jnp.where(above, xm, 0.0)
            if below is not None:
                xp = jnp.where(below, xp, 0.0)
            tap = [taps_ref[k : k + 1, lanes] for k in range(9)]
            a0 = tap[0] * xm + tap[3] * x0 + tap[6] * xp
            a1 = tap[1] * xm + tap[4] * x0 + tap[7] * xp
            a2 = tap[2] * xm + tap[5] * x0 + tap[8] * xp
            a0 = jnp.where(first, 0.0, pltpu.roll(a0, 1, 0))
            a2 = jnp.where(last, 0.0, pltpu.roll(a2, 95, 0))
            y = x0 + a1 + a0 + a2
            for t in range(CHUNKS):
                for j in range(4):
                    c = (4 * t + j) * 8
                    x_scr[t, half, j, rr, :, lanes] = y[c : c + 8]

    def inner(r, carry):
        conv_row(r, None, None)
        return carry

    lax.fori_loop(1, 15, inner, 0)

    def prepare(wqkv, load):
        load.wait()
        wk_scr[...] = wqkv[:, 512:1024]
        wqvt_scr[:512] = wqkv[:, :512].T
        wqvt_scr[512:] = wqkv[:, 1024:].T

    prepare(bqkv, loads[0])
    loads[1].wait()

    for copy in halo:
        copy.wait_recv()
    not_top, not_bottom = ri > 0, ri < 15
    conv_row(0, not_top, None)
    conv_row(15, None, not_bottom)
    row_of = lax.broadcasted_iota(jnp.int32, (16, 512), 0)
    sub = lax.broadcasted_iota(jnp.int32, (8, 512), 0)
    for cols, inside, k0, j, t, at in ((lcol, ci > 0, 0, 0, 0, 0), (rcol, ci < 7, 2, 3, 2, 7)):
        here = cols[1].astype(F32)
        before = jnp.where(not_top, cols[0].astype(F32)[15:16], 0.0)
        after = jnp.where(not_bottom, cols[2].astype(F32)[0:1], 0.0)
        shifted_m = jnp.where(row_of == 0, before, pltpu.roll(here, 1, 0))
        shifted_p = jnp.where(row_of == 15, after, pltpu.roll(here, 15, 0))
        edge = (
            taps_ref[k0 : k0 + 1, :] * shifted_m
            + taps_ref[k0 + 3 : k0 + 4, :] * here
            + taps_ref[k0 + 6 : k0 + 7, :] * shifted_p
        )
        edge = jnp.where(inside, edge, 0.0)
        for r in range(16):
            x_scr[t, r // 8, j, r % 8] += jnp.where(sub == at, edge[r : r + 1], 0.0)

    def send_all(t, src, dst, send, recv):
        def start(d, carry):
            slot, device = peer(d)
            pltpu.make_async_remote_copy(
                src.at[t, slot], dst.at[t, me], send.at[t], recv.at[t],
                device_id=device, device_id_type=MESH,
            ).start()
            return carry

        lax.fori_loop(1, PEERS, start, 0)

    def all_of(t, src, dst, send, recv):
        return pltpu.make_async_remote_copy(
            src.at[t, pl.ds(0, PEERS - 1)], dst.at[t, pl.ds(0, PEERS - 1)], send.at[t], recv.at[t],
            device_id=(ri, ci), device_id_type=MESH,
        )

    def block(t, carry):
        def rounded():
            return x_scr[t].reshape(TOK, 512).astype(BF).astype(F32)

        n_scr[...] = norm_rows(rounded(), bgain_ref[...])
        out = sublayer(n_scr, wk_scr, wqvt_scr, bwo, k_scr, qvt_scr, ot_scr)
        snd[t] = to_planes(out + rounded())
        rcv[t, me] = snd[t, me]
        send_all(t, snd, rcv, ssem, rsem)
        return carry

    lax.fori_loop(0, CHUNKS, block, 0)
    prepare(gqkv, loads[2])
    loads[3].wait()

    def grid(t, carry):
        all_of(t, snd, rcv, ssem, rsem).wait_recv()
        arrived = rcv[t].astype(F32)
        for lt in range(4):
            rows, lanes = slice(8 * (lt // 2), 8 * (lt // 2) + 8), slice(128 * (lt % 2), 128 * (lt % 2) + 128)
            g_scr[lt] = arrived[:, rows, lanes].reshape(TOK, 128)
        for q in range(8):
            window = jnp.concatenate([g_scr[lt, pl.ds(q, 64, stride=8), :] for lt in range(4)], axis=1)
            n_scr[q * 64 : (q + 1) * 64] = norm_rows(window, ggain_ref[...])
        out = sublayer(n_scr, wk_scr, wqvt_scr, gwo, k_scr, qvt_scr, ot_scr)
        for q in range(8):
            for lt in range(4):
                g_scr[lt, pl.ds(q, 64, stride=8), :] += out[q * 64 : (q + 1) * 64, lt * 128 : (lt + 1) * 128]
        snd2[t] = to_planes(jnp.concatenate([g_scr[lt] for lt in range(4)], axis=1))
        own = pltpu.make_async_copy(snd2.at[t, me], ret_ref.at[t, me], own_sem)
        own.start()
        send_all(t, snd2, ret_ref, ssem2, rsem2)
        own.wait()
        return carry

    lax.fori_loop(0, CHUNKS, grid, 0)

    for copy in halo:
        copy.wait_send()
    for t in range(CHUNKS):
        all_of(t, snd, rcv, ssem, rsem).wait_send()
    for t in range(CHUNKS):
        back = all_of(t, snd2, ret_ref, ssem2, rsem2)
        back.wait_send()
        back.wait_recv()


def unpack_kernel(ret_ref, out_ref):
    y = from_planes(ret_ref[0]).reshape(2, 4, 8, 8, 512)
    out_ref[...] = y.transpose(0, 2, 1, 3, 4).reshape(16, 32, 512).astype(BF)


def body(features, conv_taps, block_gain, block_qkv, block_out, grid_gain, grid_qkv, grid_out):
    any_ = pl.BlockSpec(memory_space=pl.ANY)
    vmem = pl.BlockSpec(memory_space=pltpu.VMEM)
    dma = pltpu.SemaphoreType.DMA
    planes = (CHUNKS, PEERS, 16, 256)
    returned = pl.pallas_call(
        main_kernel,
        out_shape=jax.ShapeDtypeStruct(planes, BF),
        in_specs=[any_, vmem, vmem, vmem, any_, any_, any_, any_],
        out_specs=any_,
        scratch_shapes=[
            pltpu.VMEM((18, 96, 512), BF),
            pltpu.VMEM((16, 512), BF),
            pltpu.VMEM((16, 512), BF),
            pltpu.VMEM((3, 16, 512), BF),
            pltpu.VMEM((3, 16, 512), BF),
            pltpu.VMEM((CHUNKS, 2, 4, 8, 8, 512), F32),
            pltpu.VMEM((4, TOK, 128), F32),
            pltpu.VMEM((512, 1536), BF),
            pltpu.VMEM((512, 1536), BF),
            pltpu.VMEM((512, 512), BF),
            pltpu.VMEM((512, 512), BF),
            pltpu.VMEM((512, 512), BF),
            pltpu.VMEM((1024, 512), BF),
            pltpu.VMEM((TOK, 512), BF),
            pltpu.VMEM((TOK, 512), BF),
            pltpu.VMEM((1024, TOK), BF),
            pltpu.VMEM((512, TOK), BF),
            pltpu.VMEM(planes, BF),
            pltpu.VMEM(planes, BF),
            pltpu.VMEM(planes, BF),
            dma((5,)),
            dma((8,)),
            dma((8,)),
            dma((CHUNKS,)),
            dma((CHUNKS,)),
            dma((CHUNKS,)),
            dma((CHUNKS,)),
            dma,
        ],
        compiler_params=pltpu.CompilerParams(
            collective_id=0, has_side_effects=True, vmem_limit_bytes=48 * 2**20
        ),
    )(
        features, conv_taps, block_gain.reshape(1, 512), grid_gain.reshape(1, 512),
        block_qkv, block_out, grid_qkv, grid_out,
    )
    return pl.pallas_call(
        unpack_kernel,
        grid=(CHUNKS,),
        out_shape=jax.ShapeDtypeStruct(features.shape, BF),
        in_specs=[pl.BlockSpec((1, PEERS, 16, 256), lambda t: (t, 0, 0, 0))],
        out_specs=pl.BlockSpec((16, 32, 512), lambda t: (0, t, 0)),
    )(returned)


def solution(mesh):
    placed = (P("rows", "cols", None), P(), P(), P(), P(), P(), P(), P())
    return jax.shard_map(
        body, mesh=mesh, in_specs=placed, out_specs=P("rows", "cols", None), check_vma=False
    )
```

time: 270 us -> 68.1 us (0.25)
  blocking collectives: 109 us -> 0 us
  Pallas kernels: 0 us -> 59.5 us
  local copies, waits for them, and re-layouts: 62.3 us -> 8.16 us
  other arithmetic: 44.3 us -> 0 us
  matrix products: 34.9 us -> 0 us
  starting transfers between devices: 10.9 us -> 0 us
  waiting for transfers between devices: 5.79 us -> 0 us
    all_to_all x4 -> x0, blocking collectives: 109 us -> none  [the longest x1 30.6 us: body(): lax.all_to_all(lax.all_to_all(sectioned, 'rows', split_axis=0, concat_axi...]
    pallas_call x0 -> x2, Pallas kernels: none -> 59.5 us  [the longest x1 56.2 us: body(): pl.pallas_call(main_kernel, out_shape=jax.ShapeDtypeStruct(planes, BF), i...]
    dot_general x8 -> x0, matrix products: 34.9 us -> none  [the longest x2 13 us: window_attention(): jnp.einsum('nhqk,nkhe->nqhe', weights_soft, values_all, preferred_element...]
    sub x2 -> x0, other arithmetic: 32.6 us -> none  [window_attention(): weights_soft = jax.nn.softmax(scores, axis=-1).astype(jnp.bfloat16)]
    reshape x5 -> x0, local copies, waits for them, and re-layouts: 28 us -> none  [the longest x2 25.2 us: window_attention(): projected.astype(jnp.bfloat16).reshape(count, length, 3, HEADS, head_dim)]
    convert_element_type x4 -> x0, local copies, waits for them, and re-layouts: 15.9 us -> none  [the longest x2 13.3 us: window_attention(): projected.astype(jnp.bfloat16).reshape(count, length, 3, HEADS, head_dim)]
    ppermute x4 -> x0, starting transfers between devices: 10.9 us -> none  [the longest x2 7.71 us: with_halo(): lax.ppermute(tail, axis, [(i, (i + 1) % count) for i in range(ends)])]
    slice x5 -> x0, local copies, waits for them, and re-layouts: 10.3 us -> none  [the longest x2 9.13 us: window_attention(): values_all = projected[:, :, 2]]
  transfers between devices with their start and end apart: 4 -> 0, of which waited for: 2 -> 0; matrix products, arithmetic and copies ran while one was open for 1% -> 0% of each run, Pallas kernels for 0% -> 0%
where the time goes in v1:
time: 68.1 us; the launch traced here: 67.7 us
  Pallas kernels  59.5 us (87%)
  local copies, waits for them, and re-layouts  8.16 us (12%)
    pallas_call x1, Pallas kernels, body(): pl.pallas_call(main_kernel, out_shape=jax.ShapeDtypeStruct(planes, BF), i...  56.2 us
    unnamed x16, local copies, waits for them, and re-layouts  8.16 us
    pallas_call x1, Pallas kernels, body(): pl.pallas_call(unpack_kernel, grid=(CHUNKS,), out_shape=jax.ShapeDtypeStr...  3.36 us

profile of v1, /device:TPU:1, one launch (start us, length us, event | category | flops | bytes accessed | tf_op | source)
XLA Modules:
  0.0 67.7 jit_solution(12281374278903446256)
XLA Ops:
  0.0 0.0 copy-start.1
  0.0 1.4 %copy-done.1 = bf16[16,96,512]{2,1,0:T(8,128)(2,1)S(1)} copy-done((bf16[16,96,512]{2,1,0:T(8,128)(2,1)S(1)}, bf16[16,96,512]{2,1,0:T(8,128)(2,1)}, u32[]{:S(2)}) %copy-start.1) | copy-done | bytes 1572888
  1.4 0.0 copy-start.2
  1.4 1.4 %copy-done.2 = bf16[512,1536]{1,0:T(8,128)(2,1)S(1)} copy-done((bf16[512,1536]{1,0:T(8,128)(2,1)S(1)}, bf16[512,1536]{1,0:T(8,128)(2,1)}, u32[]{:S(2)}) %copy-start.2) | copy-done | bytes 1572888
  2.8 0.0 copy-start.3
  2.8 1.0 %copy-done.3 = bf16[512,512]{1,0:T(8,128)(2,1)S(1)} copy-done((bf16[512,512]{1,0:T(8,128)(2,1)S(1)}, bf16[512,512]{1,0:T(8,128)(2,1)}, u32[]{:S(2)}) %copy-start.3) | copy-done | bytes 524312
  3.9 0.0 copy-start.4
  3.9 1.0 %copy-done.4 = bf16[512,512]{1,0:T(8,128)(2,1)S(1)} copy-done((bf16[512,512]{1,0:T(8,128)(2,1)S(1)}, bf16[512,512]{1,0:T(8,128)(2,1)}, u32[]{:S(2)}) %copy-start.4) | copy-done | bytes 524312
  4.9 0.0 copy-start.5
  4.9 0.8 %copy-done.5 = f32[9,512]{1,0:T(8,128)S(1)} copy-done((f32[9,512]{1,0:T(8,128)S(1)}, f32[9,512]{1,0:T(8,128)}, u32[]{:S(2)}) %copy-start.5) | copy-done | bytes 18456
  5.7 0.0 copy-start.6
  5.7 0.7 %copy-done.6 = f32[512]{0:T(512)S(1)} copy-done((f32[512]{0:T(512)S(1)}, f32[512]{0:T(512)}, u32[]{:S(2)}) %copy-start.6) | copy-done | bytes 2072
  6.3 0.0 copy-start.7
  6.3 0.7 %copy-done.7 = f32[512]{0:T(512)S(1)} copy-done((f32[512]{0:T(512)S(1)}, f32[512]{0:T(512)}, u32[]{:S(2)}) %copy-start.7) | copy-done | bytes 2072
  7.0 56.2 %shard_map.82.ret_ref = bf16[3,64,16,256]{3,2,1,0:T(8,128)(2,1)S(1)} custom-call(bf16[16,96,512]{2,1,0:T(8,128)(2,1)S(1)} %copy-done.1, f32[9,512]{1,0:T(8,128)S(1)} %copy-done.5, f32[1,512]{1,0:T(1,128)S(1)} %bitcast.2, f32[1,512]{1,0:T(1,128)S(1)} %bitcast.3, bf16[512,1536]{1,0:T(8,128)(2,1)S(1)} %copy-done.2, bf16[512,512]{1,0:T(8,128)(2,1)S(1)} %copy-done.3, ...), custom_call_target="tpu_custom_call" | custom-call | tf_op jit(solution)/shard_map/pallas_call | solution.py:314
  63.2 0.0 copy-start
  63.2 1.1 %copy-done = bf16[3,64,16,256]{3,2,1,0:T(8,128)(2,1)} copy-done((bf16[3,64,16,256]{3,2,1,0:T(8,128)(2,1)}, bf16[3,64,16,256]{3,2,1,0:T(8,128)(2,1)S(1)}, u32[]{:S(2)}) %copy-start) | copy-done | bytes 1572888
  64.3 3.4 %shard_map.83 = bf16[16,96,512]{2,1,0:T(8,128)(2,1)} custom-call(bf16[3,64,16,256]{3,2,1,0:T(8,128)(2,1)} %copy-done), custom_call_target="tpu_custom_call" | custom-call | tf_op jit(solution)/shard_map/pallas_call | solution.py:356
Async XLA Ops:
  0.0 1.4 %copy-start.1 = (bf16[16,96,512]{2,1,0:T(8,128)(2,1)S(1)}, bf16[16,96,512]{2,1,0:T(8,128)(2,1)}, u32[]{:S(2)}) copy-start(bf16[16,96,512]{2,1,0:T(8,128)(2,1)} %feat_ref.1) | copy-start | bytes 4718596
  1.4 1.4 %copy-start.2 = (bf16[512,1536]{1,0:T(8,128)(2,1)S(1)}, bf16[512,1536]{1,0:T(8,128)(2,1)}, u32[]{:S(2)}) copy-start(bf16[512,1536]{1,0:T(8,128)(2,1)} %bqkv_ref.1) | copy-start | bytes 4718596
  2.8 1.0 %copy-start.3 = (bf16[512,512]{1,0:T(8,128)(2,1)S(1)}, bf16[512,512]{1,0:T(8,128)(2,1)}, u32[]{:S(2)}) copy-start(bf16[512,512]{1,0:T(8,128)(2,1)} %bout_ref.1) | copy-start | bytes 1572868
  3.9 1.0 %copy-start.4 = (bf16[512,512]{1,0:T(8,128)(2,1)S(1)}, bf16[512,512]{1,0:T(8,128)(2,1)}, u32[]{:S(2)}) copy-start(bf16[512,512]{1,0:T(8,128)(2,1)} %gout_ref.1) | copy-start | bytes 1572868
  4.9 0.8 %copy-start.5 = (f32[9,512]{1,0:T(8,128)S(1)}, f32[9,512]{1,0:T(8,128)}, u32[]{:S(2)}) copy-start(f32[9,512]{1,0:T(8,128)} %taps_ref.1) | copy-start | bytes 55300
  5.7 0.7 %copy-start.6 = (f32[512]{0:T(512)S(1)}, f32[512]{0:T(512)}, u32[]{:S(2)}) copy-start(f32[512]{0:T(512)} %param.10) | copy-start | bytes 6148
  6.3 0.7 %copy-start.7 = (f32[512]{0:T(512)S(1)}, f32[512]{0:T(512)}, u32[]{:S(2)}) copy-start(f32[512]{0:T(512)} %param.13) | copy-start | bytes 6148
  63.2 1.1 %copy-start = (bf16[3,64,16,256]{3,2,1,0:T(8,128)(2,1)}, bf16[3,64,16,256]{3,2,1,0:T(8,128)(2,1)S(1)}, u32[]{:S(2)}) copy-start(bf16[3,64,16,256]{3,2,1,0:T(8,128)(2,1)S(1)} %shard_map.82.ret_ref) | copy-start | bytes 4718596

commit v2 on v1

v2 whole, which is shorter than its diff:
```python
import jax
import jax.numpy as jnp
from jax import lax
from jax.experimental import pallas as pl
from jax.experimental.pallas import tpu as pltpu
from jax.sharding import PartitionSpec as P

MESH = pl.DeviceIdType.MESH
BF = jnp.bfloat16
F32 = jnp.float32
HEAD_DIM = 32
SCALE = HEAD_DIM ** -0.5
PEERS = 64
PIECES = 6
TOK = 256


def mm(a, b, dims=((1,), (0,))):
    return lax.dot_general(a, b, (dims, ((), ())), preferred_element_type=F32)


def norm_rows(x, gain):
    mean = jnp.mean(x, axis=-1, keepdims=True)
    cen = x - mean
    var = jnp.mean(cen * cen, axis=-1, keepdims=True)
    return (cen * lax.rsqrt(var + 1e-5) * gain).astype(BF)


def spread_heads(q):
    cols = []
    for h in range(4):
        parts = []
        if h > 0:
            parts.append(jnp.zeros((32 * h, 128), BF))
        parts.append(q[32 * h : 32 * (h + 1)])
        if h < 3:
            parts.append(jnp.zeros((32 * (3 - h), 128), BF))
        cols.append(jnp.concatenate(parts, axis=0))
    return jnp.concatenate(cols, axis=1)


def scores(unit, k_scr, qvt_scr):
    p, g = unit
    keys = k_scr[p * 128 : (p + 1) * 128, g * 128 : (g + 1) * 128]
    q = qvt_scr[g * 128 : (g + 1) * 128, p * 128 : (p + 1) * 128]
    s4 = mm(keys, spread_heads(q))
    first = lax.broadcasted_iota(jnp.int32, (64, 128), 1) < 64
    return [
        jnp.where(first, s4[:64, h * 128 : (h + 1) * 128], s4[64:, h * 128 : (h + 1) * 128])
        for h in range(4)
    ]


def soft(heads):
    lane = lax.broadcasted_iota(jnp.int32, (64, 128), 1)
    low = jnp.where(lane < 64, 1.0, 0.0).astype(BF)
    high = jnp.where(lane < 64, 0.0, 1.0).astype(BF)
    probs, inverse = [], []
    for s in heads:
        m = jnp.max(s, axis=0, keepdims=True)
        e = jnp.exp((s - m) * SCALE)
        inverse.append(1.0 / jnp.sum(e, axis=0, keepdims=True))
        pb = e.astype(BF)
        probs.append(jnp.concatenate([pb * low, pb * high], axis=0))
    return probs, inverse


def weigh(unit, softened, qvt_scr, ot_scr):
    p, g = unit
    probs, inverse = softened
    for h in range(0, 4, 2):
        r = g * 128 + h * 32
        v2 = qvt_scr[512 + r : 512 + r + 64, p * 128 : (p + 1) * 128]
        o2 = mm(v2, jnp.concatenate([probs[h], probs[h + 1]], axis=1))
        o = jnp.concatenate([o2[:32, :128] * inverse[h], o2[32:, 128:] * inverse[h + 1]], axis=0)
        ot_scr[r : r + 64, p * 128 : (p + 1) * 128] = o.astype(BF)


def attend(pairs, k_scr, qvt_scr, ot_scr):
    units = [(p, g) for p in range(pairs) for g in range(4)]
    n, b = len(units), 2
    ready = [scores(u, k_scr, qvt_scr) for u in units[:b]]
    last = None
    for i in range(0, n, b):
        now = ready
        if i + b < n:
            ready = [scores(u, k_scr, qvt_scr) for u in units[i + b : i + 2 * b]]
        done = [soft(s) for s in now]
        if last is not None:
            for u, x in zip(units[i - b : i], last):
                weigh(u, x, qvt_scr, ot_scr)
        last = done
    for u, x in zip(units[n - b :], last):
        weigh(u, x, qvt_scr, ot_scr)


def sublayer(tokens, n_scr, wk_scr, wqvt_scr, wo_scr, k_scr, qvt_scr, ot_scr):
    normed = n_scr[:tokens]
    k_scr[:tokens] = mm(normed, wk_scr[...]).astype(BF)
    qvt_scr[:, :tokens] = mm(wqvt_scr[...], normed, ((1,), (1,))).astype(BF)
    attend(tokens // 128, k_scr, qvt_scr, ot_scr)
    return mm(ot_scr[:, :tokens], wo_scr[...], ((0,), (0,)))


def to_planes(x):
    y = x.reshape(32, 8, 512)
    upper = lax.broadcasted_iota(jnp.int32, (32, 8, 128), 1) < 4
    first, second = [], []
    for lt in range(0, 4, 2):
        a, b = y[:, :, lt * 128 : (lt + 1) * 128], y[:, :, (lt + 1) * 128 : (lt + 2) * 128]
        first.append(jnp.where(upper, a, pltpu.roll(b, 4, 1)))
        second.append(jnp.where(upper, pltpu.roll(a, 4, 1), b))
    halves = [jnp.concatenate(part, axis=1) for part in (first, second)]
    return jnp.concatenate(halves, axis=0).astype(BF)


def from_planes(planes):
    p = planes.astype(F32)
    upper = lax.broadcasted_iota(jnp.int32, (32, 8, 128), 1) < 4
    tiles = []
    for k in range(0, 16, 8):
        first, second = p[:32, k : k + 8], p[32:, k : k + 8]
        tiles.append(jnp.where(upper, first, pltpu.roll(second, 4, 1)))
        tiles.append(jnp.where(upper, pltpu.roll(first, 4, 1), second))
    return jnp.concatenate(tiles, axis=2)


def main_kernel(
    feat_ref, taps_hbm, bgain_hbm, ggain_hbm, bqkv_ref, bout_ref, gqkv_ref, gout_ref,
    ret_ref,
    taps_ref, bgain_ref, ggain_ref, fpad, coll, colr, lcol, rcol, x_scr, g_scr,
    bqkv, gqkv, bwo, gwo, wk_scr, wqvt_scr, n_scr, k_scr, qvt_scr, ot_scr,
    snd, rcv, snd2,
    local_sem, halo_send, halo_recv, ssem, rsem, ssem2, rsem2, own_sem,
):
    ri, ci = lax.axis_index("rows"), lax.axis_index("cols")
    core = lax.rem(ri, 2)
    me = (ri // 2) * 8 + ci
    up, down = lax.rem(ri + 15, 16), lax.rem(ri + 1, 16)
    left, right = lax.rem(ci + 7, 8), lax.rem(ci + 1, 8)

    def device_of(unit):
        return 2 * (unit // 8) + core, lax.rem(unit, 8)

    def peer(d):
        unit = lax.rem(me + d, PEERS)
        return unit, device_of(unit)

    barrier = pltpu.get_barrier_semaphore()

    def greet(d, carry):
        pl.semaphore_signal(barrier, inc=1, device_id=peer(d)[1], device_id_type=MESH)
        return carry

    load_feat = pltpu.make_async_copy(feat_ref, fpad.at[pl.ds(1, 16)], local_sem.at[0])
    load_feat.start()
    lax.fori_loop(1, PEERS, greet, 0)
    around = [(r, c) for r in (up, down) for c in (left, ci, right)]
    for r, c in around:
        pl.semaphore_signal(barrier, inc=1, device_id=(r, c), device_id_type=MESH)
    loads = [
        pltpu.make_async_copy(src, dst, local_sem.at[i + 1])
        for i, (src, dst) in enumerate(
            (
                (taps_hbm, taps_ref), (bgain_hbm, bgain_ref), (bqkv_ref, bqkv), (bout_ref, bwo),
                (gqkv_ref, gqkv), (gout_ref, gwo), (ggain_hbm, ggain_ref),
            )
        )
    ]
    for load in loads:
        load.start()

    load_feat.wait()
    loads[0].wait()
    for r in range(16):
        coll[r : r + 1, :] = fpad[r + 1, 0:1, :]
        colr[r : r + 1, :] = fpad[r + 1, 95:96, :]
    pl.semaphore_wait(barrier, PEERS - 1 + len(around))

    halo = [
        (fpad.at[1], fpad.at[17], (up, ci)),
        (fpad.at[16], fpad.at[0], (down, ci)),
        (coll, rcol.at[1], (ri, left)),
        (colr, lcol.at[1], (ri, right)),
        (coll, rcol.at[2], (up, left)),
        (coll, rcol.at[0], (down, left)),
        (colr, lcol.at[2], (up, right)),
        (colr, lcol.at[0], (down, right)),
    ]
    halo = [
        pltpu.make_async_remote_copy(
            src, dst, halo_send.at[i], halo_recv.at[i], device_id=to, device_id_type=MESH
        )
        for i, (src, dst, to) in enumerate(halo)
    ]
    for copy in halo:
        copy.start()
    not_top, not_bottom = ri > 0, ri < 15

    def conv_row(t, r, above, below):
        half, rr = r // 8, lax.rem(r, 8)
        c0 = 32 * t
        lo, hi = max(c0 - 16, 0), min(c0 + 48, 96)
        pre, post = 8 * (t > 0), 8 * (t < 2)
        for lt in range(4):
            lanes = slice(lt * 128, (lt + 1) * 128)
            xm = fpad[r, lo:hi, lanes].astype(F32)
            x0 = fpad[r + 1, lo:hi, lanes].astype(F32)
            xp = fpad[r + 2, lo:hi, lanes].astype(F32)
            if above is not None:
                xm = jnp.where(above, xm, 0.0)
            if below is not None:
                xp = jnp.where(below, xp, 0.0)

            def column(j, start, stop):
                k = slice(start - lo, stop - lo)
                tap = [taps_ref[i : i + 1, lanes] for i in (j, j + 3, j + 6)]
                return tap[0] * xm[k] + tap[1] * x0[k] + tap[2] * xp[k]

            a0 = pltpu.roll(column(0, c0 - pre, c0 + 32), 1, 0)
            a1 = column(1, c0, c0 + 32)
            a2 = pltpu.roll(column(2, c0, c0 + 32 + post), 31 + post, 0)
            row = lax.broadcasted_iota(jnp.int32, (32, 128), 0)
            a0 = a0[8:] if pre else jnp.where(row == 0, 0.0, a0)
            a2 = a2[:32] if post else jnp.where(row == 31, 0.0, a2)
            y = x0[c0 - lo : c0 - lo + 32] + a1 + a0 + a2
            x_scr[t, half, :, rr, :, lanes] = y.reshape(4, 8, 128)

    def conv_inner(t):
        def inner(r, carry):
            conv_row(t, r, None, None)
            return carry

        lax.fori_loop(1, 15, inner, 0)

    def conv_outer(t):
        conv_row(t, 0, not_top, None)
        conv_row(t, 15, None, not_bottom)

    def conv_side(cols, arrivals, inside, k0, j, t, at):
        for i in arrivals:
            halo[i].wait_recv()
        row_of = lax.broadcasted_iota(jnp.int32, (16, 512), 0)
        sub = lax.broadcasted_iota(jnp.int32, (8, 512), 0)
        here = cols[1].astype(F32)
        before = jnp.where(not_top, cols[0].astype(F32)[15:16], 0.0)
        after = jnp.where(not_bottom, cols[2].astype(F32)[0:1], 0.0)
        shifted_m = jnp.where(row_of == 0, before, pltpu.roll(here, 1, 0))
        shifted_p = jnp.where(row_of == 15, after, pltpu.roll(here, 15, 0))
        edge = (
            taps_ref[k0 : k0 + 1, :] * shifted_m
            + taps_ref[k0 + 3 : k0 + 4, :] * here
            + taps_ref[k0 + 6 : k0 + 7, :] * shifted_p
        )
        edge = jnp.where(inside, edge, 0.0)
        for r in range(16):
            x_scr[t, r // 8, j, r % 8] += jnp.where(sub == at, edge[r : r + 1], 0.0)

    conv_inner(1)

    def prepare(wqkv, load):
        load.wait()
        wk_scr[...] = wqkv[:, 512:1024]
        wqvt_scr[:512] = wqkv[:, :512].T
        wqvt_scr[512:] = wqkv[:, 1024:].T

    prepare(bqkv, loads[2])
    conv_inner(0)
    loads[1].wait()
    loads[3].wait()

    def send_out(i, unit):
        pltpu.make_async_remote_copy(
            snd.at[i, unit], rcv.at[i, me], ssem.at[i], rsem.at[i],
            device_id=device_of(unit), device_id_type=MESH,
        ).start()

    def send_back(i, d):
        slot, device = peer(d)
        pltpu.make_async_remote_copy(
            snd2.at[i, slot], ret_ref.at[i, me], ssem2.at[i], rsem2.at[i],
            device_id=device, device_id_type=MESH,
        ).start()

    def all_of(t, src, dst, send, recv):
        return pltpu.make_async_remote_copy(
            src.at[t, pl.ds(0, PEERS - 1)], dst.at[t, pl.ds(0, PEERS - 1)], send.at[t], recv.at[t],
            device_id=(ri, ci), device_id_type=MESH,
        )

    def block(x_ref, first, count):
        tokens = TOK * count

        def rounded():
            return x_ref[...].reshape(tokens, 512).astype(BF).astype(F32)

        n_scr[:tokens] = norm_rows(rounded(), bgain_ref[...])
        out = sublayer(tokens, n_scr, wk_scr, wqvt_scr, bwo, k_scr, qvt_scr, ot_scr) + rounded()
        for j in range(count):
            i = first + j
            snd[i] = to_planes(out[j * TOK : (j + 1) * TOK])

            def start(d, c):
                send_out(i, lax.rem(me + d, PEERS))
                return c

            lax.fori_loop(1, PEERS, start, 0, unroll=9)
            rcv[i, me] = snd[i, me]

    halo[0].wait_recv()
    halo[1].wait_recv()
    conv_outer(1)

    def middle(i, carry):
        block(x_scr.at[1, i], i, 1)
        return carry

    lax.fori_loop(0, 2, middle, 0)

    def sides(i, carry):
        @pl.when(i == 0)
        def _():
            conv_outer(0)
            conv_side(lcol, (3, 6, 7), ci > 0, 0, 0, 0, 0)

        @pl.when(i == 1)
        def _():
            conv_inner(2)
            conv_outer(2)
            conv_side(rcol, (2, 4, 5), ci < 7, 2, 3, 2, 7)

        block(x_scr.at[2 * i], 2 + 2 * i, 2)
        return carry

    lax.fori_loop(0, 2, sides, 0)
    prepare(gqkv, loads[4])
    loads[5].wait()
    loads[6].wait()

    def own(i):
        return pltpu.make_async_copy(snd2.at[i, me], ret_ref.at[i, me], own_sem.at[i])

    def grid(chunk, carry):
        def place(q, lt):
            return pl.ds(1024 * (q // 4) + 4 * lt + q % 4, PEERS, stride=16)

        for j in range(2):
            i = 2 * chunk + j
            all_of(i, snd, rcv, ssem, rsem).wait_recv()
            g_scr[j * 1024 : (j + 1) * 1024] = rcv[i].astype(F32).reshape(PEERS * 16, 128)
        for q in range(8):
            window = jnp.concatenate([g_scr[place(q, lt), :] for lt in range(4)], axis=1)
            n_scr[q * 64 : (q + 1) * 64] = norm_rows(window, ggain_ref[...])
        out = sublayer(2 * TOK, n_scr, wk_scr, wqvt_scr, gwo, k_scr, qvt_scr, ot_scr)
        for q in range(8):
            for lt in range(4):
                g_scr[place(q, lt), :] += out[q * 64 : (q + 1) * 64, lt * 128 : (lt + 1) * 128]
        for j in range(2):
            i = 2 * chunk + j
            snd2[i] = g_scr[j * 1024 : (j + 1) * 1024].reshape(PEERS, 16, 128).astype(BF)

            def start(d, c):
                send_back(i, d)
                return c

            lax.fori_loop(1, PEERS, start, 0, unroll=9)
            own(i).start()
        return carry

    lax.fori_loop(0, PIECES // 2, grid, 0)

    for copy in halo:
        copy.wait_send()
    for t in range(PIECES):
        all_of(t, snd, rcv, ssem, rsem).wait_send()
    for t in range(PIECES):
        back = all_of(t, snd2, ret_ref, ssem2, rsem2)
        back.wait_send()
        back.wait_recv()
        own(t).wait()


def unpack_kernel(ret_ref, out_ref, planes, frame, in_sem, out_sem):
    pieces = [(t, half) for t in (1, 0, 2) for half in range(2)]
    arrive = [
        pltpu.make_async_copy(ret_ref.at[i], planes.at[i], in_sem.at[i]) for i in range(PIECES)
    ]
    for copy in arrive:
        copy.start()
    leave = []
    for i, (t, half) in enumerate(pieces):
        arrive[i].wait()
        y = from_planes(planes[i]).reshape(4, 8, 8, 512).transpose(1, 0, 2, 3)
        frame[i] = y.reshape(8, 32, 512).astype(BF)
        place = out_ref.at[pl.ds(8 * half, 8), pl.ds(32 * t, 32)]
        leave.append(pltpu.make_async_copy(frame.at[i], place, out_sem.at[i]))
        leave[-1].start()
    for copy in leave:
        copy.wait()


def body(features, conv_taps, block_gain, block_qkv, block_out, grid_gain, grid_qkv, grid_out):
    any_ = pl.BlockSpec(memory_space=pl.ANY)
    dma = pltpu.SemaphoreType.DMA
    planes = (PIECES, PEERS, 16, 128)
    returned = pl.pallas_call(
        main_kernel,
        out_shape=jax.ShapeDtypeStruct(planes, BF),
        in_specs=[any_] * 8,
        out_specs=any_,
        scratch_shapes=[
            pltpu.VMEM((9, 512), F32),
            pltpu.VMEM((1, 512), F32),
            pltpu.VMEM((1, 512), F32),
            pltpu.VMEM((18, 96, 512), BF),
            pltpu.VMEM((16, 512), BF),
            pltpu.VMEM((16, 512), BF),
            pltpu.VMEM((3, 16, 512), BF),
            pltpu.VMEM((3, 16, 512), BF),
            pltpu.VMEM((3, 2, 4, 8, 8, 512), F32),
            pltpu.VMEM((2 * PEERS * 16, 128), F32),
            pltpu.VMEM((512, 1536), BF),
            pltpu.VMEM((512, 1536), BF),
            pltpu.VMEM((512, 512), BF),
            pltpu.VMEM((512, 512), BF),
            pltpu.VMEM((512, 512), BF),
            pltpu.VMEM((1024, 512), BF),
            pltpu.VMEM((2 * TOK, 512), BF),
            pltpu.VMEM((2 * TOK, 512), BF),
            pltpu.VMEM((1024, 2 * TOK), BF),
            pltpu.VMEM((512, 2 * TOK), BF),
            pltpu.VMEM(planes, BF),
            pltpu.VMEM(planes, BF),
            pltpu.VMEM(planes, BF),
            dma((8,)),
            dma((8,)),
            dma((8,)),
            dma((PIECES,)),
            dma((PIECES,)),
            dma((PIECES,)),
            dma((PIECES,)),
            dma((PIECES,)),
        ],
        compiler_params=pltpu.CompilerParams(
            collective_id=0, has_side_effects=True, vmem_limit_bytes=60 * 2**20
        ),
    )(
        features, conv_taps, block_gain.reshape(1, 512), grid_gain.reshape(1, 512),
        block_qkv, block_out, grid_qkv, grid_out,
    )
    return pl.pallas_call(
        unpack_kernel,
        out_shape=jax.ShapeDtypeStruct(features.shape, BF),
        in_specs=[any_],
        out_specs=any_,
        scratch_shapes=[
            pltpu.VMEM(planes, BF),
            pltpu.VMEM((PIECES, 8, 32, 512), BF),
            dma((PIECES,)),
            dma((PIECES,)),
        ],
        compiler_params=pltpu.CompilerParams(vmem_limit_bytes=60 * 2**20),
    )(returned)


def solution(mesh):
    placed = (P("rows", "cols", None), P(), P(), P(), P(), P(), P(), P())
    return jax.shard_map(
        body, mesh=mesh, in_specs=placed, out_specs=P("rows", "cols", None), check_vma=False
    )
```

time: 68.1 us -> 56.9 us (0.84)
  local copies, waits for them, and re-layouts: 8.16 us -> 0 us
  Pallas kernels: 59.5 us -> 56.7 us
    unnamed x16 -> x0, local copies, waits for them, and re-layouts: 8.16 us -> none
    pallas_call x1, Pallas kernels: 56.2 us -> 54.5 us  [body(): pl.pallas_call(main_kernel, out_shape=jax.ShapeDtypeStruct(planes, BF), i...]
    pallas_call x1, Pallas kernels: 3.36 us -> 2.25 us  [body(): pl.pallas_call(unpack_kernel, out_shape=jax.ShapeDtypeStruct(features.sha...]
where the time goes in v2:
time: 56.9 us; the launch traced here: 56.7 us
  Pallas kernels  56.7 us (100%)
    pallas_call x1, Pallas kernels, body(): pl.pallas_call(main_kernel, out_shape=jax.ShapeDtypeStruct(planes, BF), i...  54.5 us
    pallas_call x1, Pallas kernels, body(): pl.pallas_call(unpack_kernel, out_shape=jax.ShapeDtypeStruct(features.sha...  2.25 us

profile of v2, /device:TPU:1, one launch (start us, length us, event | category | flops | bytes accessed | tf_op | source)
XLA Modules:
  0.0 56.7 jit_solution(12245478719116524461)
XLA Ops:
  0.0 54.5 %shard_map.82.ret_ref = bf16[6,64,16,128]{3,2,1,0:T(8,128)(2,1)} custom-call(bf16[16,96,512]{2,1,0:T(8,128)(2,1)} %feat_ref.1, f32[9,512]{1,0:T(8,128)} %taps_hbm.1, f32[1,512]{1,0:T(1,128)} %bitcast.2, f32[1,512]{1,0:T(1,128)} %bitcast.3, bf16[512,1536]{1,0:T(8,128)(2,1)} %bqkv_ref.1, bf16[512,512]{1,0:T(8,128)(2,1)} %bout_ref.1, ...), custom_call_target="tpu_custom_call" | custom-call | tf_op jit(solution)/shard_map/pallas_call | solution.py:406
  54.5 2.2 %shard_map.83 = bf16[16,96,512]{2,1,0:T(8,128)(2,1)} custom-call(bf16[6,64,16,128]{3,2,1,0:T(8,128)(2,1)} %shard_map.82.ret_ref), custom_call_target="tpu_custom_call" | custom-call | tf_op jit(solution)/shard_map/pallas_call | solution.py:451

commit v3 on v2

--- a/solution.py
+++ b/solution.py
@@ -11,7 +11,7 @@
 HEAD_DIM = 32
 SCALE = HEAD_DIM ** -0.5
 PEERS = 64
-PIECES = 6
+CHUNKS = 3
 TOK = 256
 
 
@@ -178,14 +178,18 @@
     pl.semaphore_wait(barrier, PEERS - 1 + len(around))
 
     halo = [
-        (fpad.at[1], fpad.at[17], (up, ci)),
-        (fpad.at[16], fpad.at[0], (down, ci)),
+        (fpad.at[1, pl.ds(16, 64)], fpad.at[17, pl.ds(16, 64)], (up, ci)),
+        (fpad.at[16, pl.ds(16, 64)], fpad.at[0, pl.ds(16, 64)], (down, ci)),
         (coll, rcol.at[1], (ri, left)),
         (colr, lcol.at[1], (ri, right)),
         (coll, rcol.at[2], (up, left)),
         (coll, rcol.at[0], (down, left)),
         (colr, lcol.at[2], (up, right)),
         (colr, lcol.at[0], (down, right)),
+        (fpad.at[1, pl.ds(0, 16)], fpad.at[17, pl.ds(0, 16)], (up, ci)),
+        (fpad.at[16, pl.ds(0, 16)], fpad.at[0, pl.ds(0, 16)], (down, ci)),
+        (fpad.at[1, pl.ds(80, 16)], fpad.at[17, pl.ds(80, 16)], (up, ci)),
+        (fpad.at[16, pl.ds(80, 16)], fpad.at[0, pl.ds(80, 16)], (down, ci)),
     ]
     halo = [
         pltpu.make_async_remote_copy(
@@ -269,9 +273,9 @@
     loads[1].wait()
     loads[3].wait()
 
-    def send_out(i, unit):
+    def send_out(i, unit, rows):
         pltpu.make_async_remote_copy(
-            snd.at[i, unit], rcv.at[i, me], ssem.at[i], rsem.at[i],
+            snd.at[i, unit, rows], rcv.at[i, me, rows], ssem.at[i], rsem.at[i],
             device_id=device_of(unit), device_id_type=MESH,
         ).start()
 
@@ -288,7 +292,7 @@
             device_id=(ri, ci), device_id_type=MESH,
         )
 
-    def block(x_ref, first, count):
+    def block(x_ref, i, count, row):
         tokens = TOK * count
 
         def rounded():
@@ -297,22 +301,23 @@
         n_scr[:tokens] = norm_rows(rounded(), bgain_ref[...])
         out = sublayer(tokens, n_scr, wk_scr, wqvt_scr, bwo, k_scr, qvt_scr, ot_scr) + rounded()
         for j in range(count):
-            i = first + j
-            snd[i] = to_planes(out[j * TOK : (j + 1) * TOK])
-
-            def start(d, c):
-                send_out(i, lax.rem(me + d, PEERS))
-                return c
-
-            lax.fori_loop(1, PEERS, start, 0, unroll=9)
-            rcv[i, me] = snd[i, me]
-
+            snd[i, :, pl.ds(row + 16 * j, 16), :] = to_planes(out[j * TOK : (j + 1) * TOK])
+        rows = pl.ds(row, 16 * count)
+
+        def start(d, c):
+            send_out(i, lax.rem(me + d, PEERS), rows)
+            return c
+
+        lax.fori_loop(1, PEERS, start, 0, unroll=9)
+        rcv[i, me, rows, :] = snd[i, me, rows, :]
+
+    conv_inner(2)
     halo[0].wait_recv()
     halo[1].wait_recv()
     conv_outer(1)
 
     def middle(i, carry):
-        block(x_scr.at[1, i], i, 1)
+        block(x_scr.at[1, i], 0, 1, pl.multiple_of(16 * i, 16))
         return carry
 
     lax.fori_loop(0, 2, middle, 0)
@@ -320,16 +325,19 @@
     def sides(i, carry):
         @pl.when(i == 0)
         def _():
+            halo[8].wait_recv()
+            halo[9].wait_recv()
             conv_outer(0)
             conv_side(lcol, (3, 6, 7), ci > 0, 0, 0, 0, 0)
 
         @pl.when(i == 1)
         def _():
-            conv_inner(2)
+            halo[10].wait_recv()
+            halo[11].wait_recv()
             conv_outer(2)
             conv_side(rcol, (2, 4, 5), ci < 7, 2, 3, 2, 7)
 
-        block(x_scr.at[2 * i], 2 + 2 * i, 2)
+        block(x_scr.at[2 * i], 1 + i, 2, 0)
         return carry
 
     lax.fori_loop(0, 2, sides, 0)
@@ -340,14 +348,12 @@
     def own(i):
         return pltpu.make_async_copy(snd2.at[i, me], ret_ref.at[i, me], own_sem.at[i])
 
-    def grid(chunk, carry):
+    def grid(i, carry):
         def place(q, lt):
-            return pl.ds(1024 * (q // 4) + 4 * lt + q % 4, PEERS, stride=16)
-
-        for j in range(2):
-            i = 2 * chunk + j
-            all_of(i, snd, rcv, ssem, rsem).wait_recv()
-            g_scr[j * 1024 : (j + 1) * 1024] = rcv[i].astype(F32).reshape(PEERS * 16, 128)
+            return pl.ds(16 * (q // 4) + 4 * lt + q % 4, PEERS, stride=32)
+
+        all_of(i, snd, rcv, ssem, rsem).wait_recv()
+        g_scr[...] = rcv[i].astype(F32).reshape(PEERS * 32, 128)
         for q in range(8):
             window = jnp.concatenate([g_scr[place(q, lt), :] for lt in range(4)], axis=1)
             n_scr[q * 64 : (q + 1) * 64] = norm_rows(window, ggain_ref[...])
@@ -355,43 +361,34 @@
         for q in range(8):
             for lt in range(4):
                 g_scr[place(q, lt), :] += out[q * 64 : (q + 1) * 64, lt * 128 : (lt + 1) * 128]
-        for j in range(2):
-            i = 2 * chunk + j
-            snd2[i] = g_scr[j * 1024 : (j + 1) * 1024].reshape(PEERS, 16, 128).astype(BF)
-
-            def start(d, c):
-                send_back(i, d)
-                return c
-
-            lax.fori_loop(1, PEERS, start, 0, unroll=9)
-            own(i).start()
+        snd2[i] = g_scr[...].reshape(PEERS, 32, 128).astype(BF)
+
+        def start(d, c):
+            send_back(i, d)
+            return c
+
+        lax.fori_loop(1, PEERS, start, 0, unroll=9)
+        own(i).start()
         return carry
 
-    lax.fori_loop(0, PIECES // 2, grid, 0)
+    lax.fori_loop(0, CHUNKS, grid, 0)
 
     for copy in halo:
         copy.wait_send()
-    for t in range(PIECES):
+    for t in range(CHUNKS):
         all_of(t, snd, rcv, ssem, rsem).wait_send()
-    for t in range(PIECES):
+    for t in range(CHUNKS):
         back = all_of(t, snd2, ret_ref, ssem2, rsem2)
         back.wait_send()
         back.wait_recv()
         own(t).wait()
 
 
-def unpack_kernel(ret_ref, out_ref, planes, frame, in_sem, out_sem):
-    pieces = [(t, half) for t in (1, 0, 2) for half in range(2)]
-    arrive = [
-        pltpu.make_async_copy(ret_ref.at[i], planes.at[i], in_sem.at[i]) for i in range(PIECES)
-    ]
-    for copy in arrive:
-        copy.start()
+def unpack_kernel(ret_ref, out_ref, frame, out_sem):
     leave = []
-    for i, (t, half) in enumerate(pieces):
-        arrive[i].wait()
-        y = from_planes(planes[i]).reshape(4, 8, 8, 512).transpose(1, 0, 2, 3)
-        frame[i] = y.reshape(8, 32, 512).astype(BF)
+    for i, (t, half) in enumerate([(t, half) for t in (1, 0, 2) for half in range(2)]):
+        y = from_planes(ret_ref[i // 2, :, 16 * half : 16 * half + 16, :]).reshape(4, 8, 8, 512)
+        frame[i] = y.transpose(1, 0, 2, 3).reshape(8, 32, 512).astype(BF)
         place = out_ref.at[pl.ds(8 * half, 8), pl.ds(32 * t, 32)]
         leave.append(pltpu.make_async_copy(frame.at[i], place, out_sem.at[i]))
         leave[-1].start()
@@ -401,13 +398,14 @@
 
 def body(features, conv_taps, block_gain, block_qkv, block_out, grid_gain, grid_qkv, grid_out):
     any_ = pl.BlockSpec(memory_space=pl.ANY)
+    vmem = pl.BlockSpec(memory_space=pltpu.VMEM)
     dma = pltpu.SemaphoreType.DMA
-    planes = (PIECES, PEERS, 16, 128)
+    planes = (CHUNKS, PEERS, 32, 128)
     returned = pl.pallas_call(
         main_kernel,
-        out_shape=jax.ShapeDtypeStruct(planes, BF),
+        out_shape=pltpu.VMEM(planes, BF),
         in_specs=[any_] * 8,
-        out_specs=any_,
+        out_specs=vmem,
         scratch_shapes=[
             pltpu.VMEM((9, 512), F32),
             pltpu.VMEM((1, 512), F32),
@@ -433,13 +431,13 @@
             pltpu.VMEM(planes, BF),
             pltpu.VMEM(planes, BF),
             dma((8,)),
-            dma((8,)),
-            dma((8,)),
-            dma((PIECES,)),
-            dma((PIECES,)),
-            dma((PIECES,)),
-            dma((PIECES,)),
-            dma((PIECES,)),
+            dma((12,)),
+            dma((12,)),
+            dma((CHUNKS,)),
+            dma((CHUNKS,)),
+            dma((CHUNKS,)),
+            dma((CHUNKS,)),
+            dma((CHUNKS,)),
         ],
         compiler_params=pltpu.CompilerParams(
             collective_id=0, has_side_effects=True, vmem_limit_bytes=60 * 2**20
@@ -451,15 +449,13 @@
     return pl.pallas_call(
         unpack_kernel,
         out_shape=jax.ShapeDtypeStruct(features.shape, BF),
-        in_specs=[any_],
+        in_specs=[vmem],
         out_specs=any_,
         scratch_shapes=[
-            pltpu.VMEM(planes, BF),
-            pltpu.VMEM((PIECES, 8, 32, 512), BF),
-            dma((PIECES,)),
-            dma((PIECES,)),
+            pltpu.VMEM((2 * CHUNKS, 8, 32, 512), BF),
+            dma((2 * CHUNKS,)),
         ],
-        compiler_params=pltpu.CompilerParams(vmem_limit_bytes=60 * 2**20),
+        compiler_params=pltpu.CompilerParams(vmem_limit_bytes=16 * 2**20),
     )(returned)
 
 

time: 56.9 us -> 56.1 us (0.986)
  Pallas kernels: 56.7 us -> 55.9 us
    pallas_call x1, Pallas kernels: 2.25 us -> 1.25 us  [body(): pl.pallas_call(unpack_kernel, out_shape=jax.ShapeDtypeStruct(features.sha...]
where the time goes in v3:
time: 56.1 us; the launch traced here: 55.9 us
  Pallas kernels  55.9 us (100%)
    pallas_call x1, Pallas kernels, body(): pl.pallas_call(main_kernel, out_shape=pltpu.VMEM(planes, BF), in_specs=[a...  54.7 us
    pallas_call x1, Pallas kernels, body(): pl.pallas_call(unpack_kernel, out_shape=jax.ShapeDtypeStruct(features.sha...  1.25 us

profile of v3, /device:TPU:1, one launch (start us, length us, event | category | flops | bytes accessed | tf_op | source)
XLA Modules:
  0.0 55.9 jit_solution(17611485794807561201)
XLA Ops:
  0.0 54.7 %shard_map.82.ret_ref = bf16[3,64,32,128]{3,2,1,0:T(8,128)(2,1)S(1)} custom-call(bf16[16,96,512]{2,1,0:T(8,128)(2,1)} %feat_ref.1, f32[9,512]{1,0:T(8,128)} %taps_hbm.1, f32[1,512]{1,0:T(1,128)} %bitcast.2, f32[1,512]{1,0:T(1,128)} %bitcast.3, bf16[512,1536]{1,0:T(8,128)(2,1)} %bqkv_ref.1, bf16[512,512]{1,0:T(8,128)(2,1)} %bout_ref.1, ...), custom_call_target="tpu_custom_call" | custom-call | tf_op jit(solution)/shard_map/pallas_call | solution.py:404
  54.7 1.2 %shard_map.83 = bf16[16,96,512]{2,1,0:T(8,128)(2,1)} custom-call(bf16[3,64,32,128]{3,2,1,0:T(8,128)(2,1)S(1)} %shard_map.82.ret_ref), custom_call_target="tpu_custom_call" | custom-call | tf_op jit(solution)/shard_map/pallas_call | solution.py:449

commit v4 on v3

--- a/solution.py
+++ b/solution.py
@@ -76,13 +76,32 @@
         ot_scr[r : r + 64, p * 128 : (p + 1) * 128] = o.astype(BF)
 
 
-def attend(pairs, k_scr, qvt_scr, ot_scr):
-    units = [(p, g) for p in range(pairs) for g in range(4)]
-    n, b = len(units), 2
+def sublayer(tokens, n_scr, wk_scr, wqvt_scr, wo_scr, k_scr, qvt_scr, ot_scr):
+    tok = slice(0, tokens)
+    normed = n_scr[tok]
+
+    def project(first, size):
+        rows = slice(first, first + size)
+        qvt_scr[rows, tok] = mm(wqvt_scr[rows], normed, ((1,), (1,))).astype(BF)
+
+    def keys(first):
+        cols = slice(first, first + 256)
+        k_scr[tok, cols] = mm(normed, wk_scr[:, cols]).astype(BF)
+
+    pairs, b = tokens // 128, 2
+    units = [(p, g) for half in range(2) for p in range(pairs) for g in (2 * half, 2 * half + 1)]
+    n = len(units)
+    keys(0)
+    project(0, 256)
     ready = [scores(u, k_scr, qvt_scr) for u in units[:b]]
-    last = None
+    project(512, 256)
+    last, later = None, [lambda: keys(256), lambda: project(256, 256), lambda: project(768, 256)]
+    out = None
     for i in range(0, n, b):
         now = ready
+        if i // b >= n // (2 * b) - len(later) - 1:
+            while later and i // b >= n // (2 * b) - len(later) - 1:
+                later.pop(0)()
         if i + b < n:
             ready = [scores(u, k_scr, qvt_scr) for u in units[i + b : i + 2 * b]]
         done = [soft(s) for s in now]
@@ -90,16 +109,11 @@
             for u, x in zip(units[i - b : i], last):
                 weigh(u, x, qvt_scr, ot_scr)
         last = done
+        if i == n // 2 + b:
+            out = mm(ot_scr[:256, tok], wo_scr[:256], ((0,), (0,)))
     for u, x in zip(units[n - b :], last):
         weigh(u, x, qvt_scr, ot_scr)
-
-
-def sublayer(tokens, n_scr, wk_scr, wqvt_scr, wo_scr, k_scr, qvt_scr, ot_scr):
-    normed = n_scr[:tokens]
-    k_scr[:tokens] = mm(normed, wk_scr[...]).astype(BF)
-    qvt_scr[:, :tokens] = mm(wqvt_scr[...], normed, ((1,), (1,))).astype(BF)
-    attend(tokens // 128, k_scr, qvt_scr, ot_scr)
-    return mm(ot_scr[:, :tokens], wo_scr[...], ((0,), (0,)))
+    return out + mm(ot_scr[256:, tok], wo_scr[256:], ((0,), (0,)))
 
 
 def to_planes(x):
@@ -129,7 +143,7 @@
     feat_ref, taps_hbm, bgain_hbm, ggain_hbm, bqkv_ref, bout_ref, gqkv_ref, gout_ref,
     ret_ref,
     taps_ref, bgain_ref, ggain_ref, fpad, coll, colr, lcol, rcol, x_scr, g_scr,
-    bqkv, gqkv, bwo, gwo, wk_scr, wqvt_scr, n_scr, k_scr, qvt_scr, ot_scr,
+    bqkv, gqkv, bwo, gwo, wk_scr, wqvt_scr, n_scr, n_mid, k_scr, qvt_scr, ot_scr,
     snd, rcv, snd2,
     local_sem, halo_send, halo_recv, ssem, rsem, ssem2, rsem2, own_sem,
 ):
@@ -292,14 +306,16 @@
             device_id=(ri, ci), device_id_type=MESH,
         )
 
-    def block(x_ref, i, count, row):
+    def block(x_ref, normed, i, count, row):
         tokens = TOK * count
 
         def rounded():
             return x_ref[...].reshape(tokens, 512).astype(BF).astype(F32)
 
-        n_scr[:tokens] = norm_rows(rounded(), bgain_ref[...])
-        out = sublayer(tokens, n_scr, wk_scr, wqvt_scr, bwo, k_scr, qvt_scr, ot_scr) + rounded()
+        if normed is None:
+            normed = n_scr
+            normed[...] = norm_rows(rounded(), bgain_ref[...])
+        out = sublayer(tokens, normed, wk_scr, wqvt_scr, bwo, k_scr, qvt_scr, ot_scr) + rounded()
         for j in range(count):
             snd[i, :, pl.ds(row + 16 * j, 16), :] = to_planes(out[j * TOK : (j + 1) * TOK])
         rows = pl.ds(row, 16 * count)
@@ -311,13 +327,20 @@
         lax.fori_loop(1, PEERS, start, 0, unroll=9)
         rcv[i, me, rows, :] = snd[i, me, rows, :]
 
-    conv_inner(2)
+    for half in range(2):
+        x = x_scr[1, half].reshape(TOK, 512).astype(BF).astype(F32)
+        n_mid[half] = norm_rows(x, bgain_ref[...])
     halo[0].wait_recv()
     halo[1].wait_recv()
     conv_outer(1)
+    for half, r in ((0, 0), (1, 6)):
+        x = x_scr[1, half, :, r : r + 2].reshape(64, 512).astype(BF).astype(F32)
+        again = norm_rows(x, bgain_ref[...])
+        for j in range(4):
+            n_mid[half, 64 * j + 8 * r : 64 * j + 8 * r + 16, :] = again[16 * j : 16 * j + 16]
 
     def middle(i, carry):
-        block(x_scr.at[1, i], 0, 1, pl.multiple_of(16 * i, 16))
+        block(x_scr.at[1, i], n_mid.at[i], 0, 1, pl.multiple_of(16 * i, 16))
         return carry
 
     lax.fori_loop(0, 2, middle, 0)
@@ -334,10 +357,11 @@
         def _():
             halo[10].wait_recv()
             halo[11].wait_recv()
+            conv_inner(2)
             conv_outer(2)
             conv_side(rcol, (2, 4, 5), ci < 7, 2, 3, 2, 7)
 
-        block(x_scr.at[2 * i], 1 + i, 2, 0)
+        block(x_scr.at[2 * i], None, 1 + i, 2, 0)
         return carry
 
     lax.fori_loop(0, 2, sides, 0)
@@ -424,6 +448,7 @@
             pltpu.VMEM((512, 512), BF),
             pltpu.VMEM((1024, 512), BF),
             pltpu.VMEM((2 * TOK, 512), BF),
+            pltpu.VMEM((2, TOK, 512), BF),
             pltpu.VMEM((2 * TOK, 512), BF),
             pltpu.VMEM((1024, 2 * TOK), BF),
             pltpu.VMEM((512, 2 * TOK), BF),

time: 56.1 us -> 55.3 us (0.986)
  Pallas kernels: 55.9 us -> 55.2 us
    pallas_call x1, Pallas kernels: 54.7 us -> 54 us  [body(): pl.pallas_call(main_kernel, out_shape=pltpu.VMEM(planes, BF), in_specs=[a...]
where the time goes in v4:
time: 55.3 us; the launch traced here: 55.2 us
  Pallas kernels  55.2 us (100%)
    pallas_call x1, Pallas kernels, body(): pl.pallas_call(main_kernel, out_shape=pltpu.VMEM(planes, BF), in_specs=[a...  54 us
    pallas_call x1, Pallas kernels, body(): pl.pallas_call(unpack_kernel, out_shape=jax.ShapeDtypeStruct(features.sha...  1.25 us

profile of v4, /device:TPU:1, one launch (start us, length us, event | category | flops | bytes accessed | tf_op | source)
XLA Modules:
  0.0 55.2 jit_solution(3720109089964823259)
XLA Ops:
  0.0 54.0 %shard_map.82.ret_ref = bf16[3,64,32,128]{3,2,1,0:T(8,128)(2,1)S(1)} custom-call(bf16[16,96,512]{2,1,0:T(8,128)(2,1)} %feat_ref.1, f32[9,512]{1,0:T(8,128)} %taps_hbm.1, f32[1,512]{1,0:T(1,128)} %bitcast.2, f32[1,512]{1,0:T(1,128)} %bitcast.3, bf16[512,1536]{1,0:T(8,128)(2,1)} %bqkv_ref.1, bf16[512,512]{1,0:T(8,128)(2,1)} %bout_ref.1, ...), custom_call_target="tpu_custom_call" | custom-call | tf_op jit(solution)/shard_map/pallas_call | solution.py:428
  54.0 1.2 %shard_map.83 = bf16[16,96,512]{2,1,0:T(8,128)(2,1)} custom-call(bf16[3,64,32,128]{3,2,1,0:T(8,128)(2,1)S(1)} %shard_map.82.ret_ref), custom_call_target="tpu_custom_call" | custom-call | tf_op jit(solution)/shard_map/pallas_call | solution.py:474

commit v5 on v4

--- a/solution.py
+++ b/solution.py
@@ -166,9 +166,14 @@
         pl.semaphore_signal(barrier, inc=1, device_id=peer(d)[1], device_id_type=MESH)
         return carry
 
-    load_feat = pltpu.make_async_copy(feat_ref, fpad.at[pl.ds(1, 16)], local_sem.at[0])
+    load_edge = [
+        pltpu.make_async_copy(feat_ref.at[r], fpad.at[r + 1], local_sem.at[8 + i]) for i, r in enumerate((0, 15))
+    ]
+    load_feat = pltpu.make_async_copy(feat_ref.at[pl.ds(1, 14)], fpad.at[pl.ds(2, 14)], local_sem.at[0])
+    for load in load_edge:
+        load.start()
     load_feat.start()
-    lax.fori_loop(1, PEERS, greet, 0)
+    lax.fori_loop(1, PEERS, greet, 0, unroll=9)
     around = [(r, c) for r in (up, down) for c in (left, ci, right)]
     for r, c in around:
         pl.semaphore_signal(barrier, inc=1, device_id=(r, c), device_id_type=MESH)
@@ -184,11 +189,8 @@
     for load in loads:
         load.start()
 
-    load_feat.wait()
-    loads[0].wait()
-    for r in range(16):
-        coll[r : r + 1, :] = fpad[r + 1, 0:1, :]
-        colr[r : r + 1, :] = fpad[r + 1, 95:96, :]
+    for load in load_edge:
+        load.wait()
     pl.semaphore_wait(barrier, PEERS - 1 + len(around))
 
     halo = [
@@ -211,7 +213,14 @@
         )
         for i, (src, dst, to) in enumerate(halo)
     ]
-    for copy in halo:
+    for copy in halo[:2]:
+        copy.start()
+    load_feat.wait()
+    loads[0].wait()
+    for r in range(16):
+        coll[r : r + 1, :] = fpad[r + 1, 0:1, :]
+        colr[r : r + 1, :] = fpad[r + 1, 95:96, :]
+    for copy in halo[2:]:
         copy.start()
     not_top, not_bottom = ri > 0, ri < 15
 
@@ -330,16 +339,27 @@
     for half in range(2):
         x = x_scr[1, half].reshape(TOK, 512).astype(BF).astype(F32)
         n_mid[half] = norm_rows(x, bgain_ref[...])
-    halo[0].wait_recv()
-    halo[1].wait_recv()
-    conv_outer(1)
-    for half, r in ((0, 0), (1, 6)):
+
+    def norm_again(half, r):
         x = x_scr[1, half, :, r : r + 2].reshape(64, 512).astype(BF).astype(F32)
         again = norm_rows(x, bgain_ref[...])
         for j in range(4):
             n_mid[half, 64 * j + 8 * r : 64 * j + 8 * r + 16, :] = again[16 * j : 16 * j + 16]
 
+
     def middle(i, carry):
+        @pl.when(i == 0)
+        def _():
+            halo[1].wait_recv()
+            conv_row(1, 0, not_top, None)
+            norm_again(0, 0)
+
+        @pl.when(i == 1)
+        def _():
+            halo[0].wait_recv()
+            conv_row(1, 15, None, not_bottom)
+            norm_again(1, 6)
+
         block(x_scr.at[1, i], n_mid.at[i], 0, 1, pl.multiple_of(16 * i, 16))
         return carry
 
@@ -455,7 +475,7 @@
             pltpu.VMEM(planes, BF),
             pltpu.VMEM(planes, BF),
             pltpu.VMEM(planes, BF),
-            dma((8,)),
+            dma((10,)),
             dma((12,)),
             dma((12,)),
             dma((CHUNKS,)),

time: 55.3 us -> 54.6 us (0.987)
  Pallas kernels: 55.2 us -> 54.5 us
    pallas_call x1, Pallas kernels: 54 us -> 53.3 us  [body(): pl.pallas_call(main_kernel, out_shape=pltpu.VMEM(planes, BF), in_specs=[a...]
where the time goes in v5:
time: 54.6 us; the launch traced here: 54.5 us
  Pallas kernels  54.5 us (100%)
    pallas_call x1, Pallas kernels, body(): pl.pallas_call(main_kernel, out_shape=pltpu.VMEM(planes, BF), in_specs=[a...  53.3 us
    pallas_call x1, Pallas kernels, body(): pl.pallas_call(unpack_kernel, out_shape=jax.ShapeDtypeStruct(features.sha...  1.25 us

profile of v5, /device:TPU:1, one launch (start us, length us, event | category | flops | bytes accessed | tf_op | source)
XLA Modules:
  0.0 54.5 jit_solution(8101016052243118669)
XLA Ops:
  0.0 53.3 %shard_map.82.ret_ref = bf16[3,64,32,128]{3,2,1,0:T(8,128)(2,1)S(1)} custom-call(bf16[16,96,512]{2,1,0:T(8,128)(2,1)} %feat_ref.1, f32[9,512]{1,0:T(8,128)} %taps_hbm.1, f32[1,512]{1,0:T(1,128)} %bitcast.2, f32[1,512]{1,0:T(1,128)} %bitcast.3, bf16[512,1536]{1,0:T(8,128)(2,1)} %bqkv_ref.1, bf16[512,512]{1,0:T(8,128)(2,1)} %bout_ref.1, ...), custom_call_target="tpu_custom_call" | custom-call | tf_op jit(solution)/shard_map/pallas_call | solution.py:448
  53.3 1.2 %shard_map.83 = bf16[16,96,512]{2,1,0:T(8,128)(2,1)} custom-call(bf16[3,64,32,128]{3,2,1,0:T(8,128)(2,1)S(1)} %shard_map.82.ret_ref), custom_call_target="tpu_custom_call" | custom-call | tf_op jit(solution)/shard_map/pallas_call | solution.py:494

commit v6 on v5

--- a/solution.py
+++ b/solution.py
@@ -74,6 +74,32 @@
         o2 = mm(v2, jnp.concatenate([probs[h], probs[h + 1]], axis=1))
         o = jnp.concatenate([o2[:32, :128] * inverse[h], o2[32:, 128:] * inverse[h + 1]], axis=0)
         ot_scr[r : r + 64, p * 128 : (p + 1) * 128] = o.astype(BF)
+
+
+def attend(pairs, k_scr, qvt_scr, ot_scr):
+    units = [(p, g) for p in range(pairs) for g in range(4)]
+    n, b = len(units), 2
+    ready = [scores(u, k_scr, qvt_scr) for u in units[:b]]
+    last = None
+    for i in range(0, n, b):
+        now = ready
+        if i + b < n:
+            ready = [scores(u, k_scr, qvt_scr) for u in units[i + b : i + 2 * b]]
+        done = [soft(s) for s in now]
+        if last is not None:
+            for u, x in zip(units[i - b : i], last):
+                weigh(u, x, qvt_scr, ot_scr)
+        last = done
+    for u, x in zip(units[n - b :], last):
+        weigh(u, x, qvt_scr, ot_scr)
+
+
+def sublayer_whole(tokens, n_scr, wk_scr, wqvt_scr, wo_scr, k_scr, qvt_scr, ot_scr):
+    normed = n_scr[:tokens]
+    k_scr[:tokens] = mm(normed, wk_scr[...]).astype(BF)
+    qvt_scr[:, :tokens] = mm(wqvt_scr[...], normed, ((1,), (1,))).astype(BF)
+    attend(tokens // 128, k_scr, qvt_scr, ot_scr)
+    return mm(ot_scr[:, :tokens], wo_scr[...], ((0,), (0,)))
 
 
 def sublayer(tokens, n_scr, wk_scr, wqvt_scr, wo_scr, k_scr, qvt_scr, ot_scr):
@@ -213,8 +239,8 @@
         )
         for i, (src, dst, to) in enumerate(halo)
     ]
-    for copy in halo[:2]:
-        copy.start()
+    halo[1].start()
+    halo[0].start()
     load_feat.wait()
     loads[0].wait()
     for r in range(16):
@@ -324,7 +350,8 @@
         if normed is None:
             normed = n_scr
             normed[...] = norm_rows(rounded(), bgain_ref[...])
-        out = sublayer(tokens, normed, wk_scr, wqvt_scr, bwo, k_scr, qvt_scr, ot_scr) + rounded()
+        apply = sublayer if count == 1 else sublayer_whole
+        out = apply(tokens, normed, wk_scr, wqvt_scr, bwo, k_scr, qvt_scr, ot_scr) + rounded()
         for j in range(count):
             snd[i, :, pl.ds(row + 16 * j, 16), :] = to_planes(out[j * TOK : (j + 1) * TOK])
         rows = pl.ds(row, 16 * count)
@@ -401,7 +428,7 @@
         for q in range(8):
             window = jnp.concatenate([g_scr[place(q, lt), :] for lt in range(4)], axis=1)
             n_scr[q * 64 : (q + 1) * 64] = norm_rows(window, ggain_ref[...])
-        out = sublayer(2 * TOK, n_scr, wk_scr, wqvt_scr, gwo, k_scr, qvt_scr, ot_scr)
+        out = sublayer_whole(2 * TOK, n_scr, wk_scr, wqvt_scr, gwo, k_scr, qvt_scr, ot_scr)
         for q in range(8):
             for lt in range(4):
                 g_scr[place(q, lt), :] += out[q * 64 : (q + 1) * 64, lt * 128 : (lt + 1) * 128]

time: 54.6 us -> 54.5 us (level)
  no operation moved by 1% of the time
where the time goes in v6:
time: 54.5 us; the launch traced here: 54.4 us
  Pallas kernels  54.3 us (100%)
    pallas_call x1, Pallas kernels, body(): pl.pallas_call(main_kernel, out_shape=pltpu.VMEM(planes, BF), in_specs=[a...  53.1 us
    pallas_call x1, Pallas kernels, body(): pl.pallas_call(unpack_kernel, out_shape=jax.ShapeDtypeStruct(features.sha...  1.25 us

profile of v6, /device:TPU:1, one launch (start us, length us, event | category | flops | bytes accessed | tf_op | source)
XLA Modules:
  0.0 54.4 jit_solution(10931227292535717298)
XLA Ops:
  0.0 53.1 %shard_map.82.ret_ref = bf16[3,64,32,128]{3,2,1,0:T(8,128)(2,1)S(1)} custom-call(bf16[16,96,512]{2,1,0:T(8,128)(2,1)} %feat_ref.1, f32[9,512]{1,0:T(8,128)} %taps_hbm.1, f32[1,512]{1,0:T(1,128)} %bitcast.2, f32[1,512]{1,0:T(1,128)} %bitcast.3, bf16[512,1536]{1,0:T(8,128)(2,1)} %bqkv_ref.1, bf16[512,512]{1,0:T(8,128)(2,1)} %bout_ref.1, ...), custom_call_target="tpu_custom_call" | custom-call | tf_op jit(solution)/shard_map/pallas_call | solution.py:475
  53.1 1.2 %shard_map.83 = bf16[16,96,512]{2,1,0:T(8,128)(2,1)} custom-call(bf16[3,64,32,128]{3,2,1,0:T(8,128)(2,1)S(1)} %shard_map.82.ret_ref), custom_call_target="tpu_custom_call" | custom-call | tf_op jit(solution)/shard_map/pallas_call | solution.py:521
